TPU v7x, 128 devices: a whole 4x4x4 slice. The times are simulated.
128 devices in a mesh: curve: 128 (over x, y, z, core).
Axes of the slice: x: 4, y: 4, z: 4, core: 2. Of those that a mesh axis runs over, the one named last changes fastest.
Arguments:
- fields: float32 [2, 16, 16, 16, 8192], P(None, None, None, None, 'curve'), may hold values from -1 to 1
- weights: int32 [8192], P('curve'), may hold values from 1 to 24, as said below
- levels: int32 [8192], P('curve'), may hold values from 0 to 1
- neighbours: int32 [6, 8192], P(None, 'curve'), may hold values from -1 to 8191, as said below
Outputs:
- new_fields: float32 [2, 16, 16, 16, 16384], P(None, None, None, None, 'curve')
Inputs may be any that keep to these rules, and one draw needn't show every extreme that they name: `weights`: under the steps' rule every block's new owner is its old owner or a rank beside it; at most 32 blocks pass between two ranks beside each other in either direction, and the blocks of every new owner have the same weight sum. `neighbours`: every entry is -1 or a block at most 16 positions away along the curve.
All inputs are finite; a program needn't handle non-finite values.
Results may differ from a plain program's by a relative error of at most 0.0003.
Values sent between devices are 32-bit elements; how exact they have to be, the bound alone decides.
A program may use at most 128 MiB of HBM per device.

v0:
```python
import jax
import jax.numpy as jnp
from jax import lax
from jax.sharding import PartitionSpec as P

MOBILITY_STEP = 0.0006
STIFFNESS = 1.0
COUPLING = 0.5
DIFFUSE_STEP = 0.01
SEGREGATE = 0.5


def with_halo(cells, sides, width):
    for axis, dim in sides:
        count = lax.axis_size(axis)
        ends = count - 1
        head = lax.slice_in_dim(cells, 0, width, axis=dim)
        tail = lax.slice_in_dim(cells, cells.shape[dim] - width, cells.shape[dim], axis=dim)
        cells = jnp.concatenate(
            [
                lax.ppermute(tail, axis, [(i, (i + 1) % count) for i in range(ends)]),
                cells,
                lax.ppermute(head, axis, [((i + 1) % count, i) for i in range(ends)]),
            ],
            axis=dim,
        )
    return cells


def prefix(array, axis, combine, identity):
    peers, mine = (lax.axis_size(axis), lax.axis_index(axis))
    everything = lax.all_gather(array, axis)
    start = jnp.broadcast_to(jnp.asarray(identity, array.dtype), array.shape)

    def step(k, before):
        reached = k < mine
        new = combine(before, everything[k])
        return jnp.where(reached, new, before)

    return lax.fori_loop(0, peers, step, start)


def face_table(current):
    order_field = current[0]
    surf_field = current[1]
    last_cell = order_field.shape[0] - 1
    return jnp.stack(
        [
            jnp.stack([order_field[0], order_field[1], surf_field[0]]),
            jnp.stack([order_field[last_cell], order_field[last_cell - 1], surf_field[last_cell]]),
            jnp.stack([order_field[:, 0], order_field[:, 1], surf_field[:, 0]]),
            jnp.stack(
                [order_field[:, last_cell], order_field[:, last_cell - 1], surf_field[:, last_cell]]
            ),
            jnp.stack([order_field[:, :, 0], order_field[:, :, 1], surf_field[:, :, 0]]),
            jnp.stack(
                [
                    order_field[:, :, last_cell],
                    order_field[:, :, last_cell - 1],
                    surf_field[:, :, last_cell],
                ]
            ),
        ]
    )


def ghosts(ext_table, lookup, neighbour_ids, own_faces):
    ghost_sets = []
    for face_idx in range(6):
        picked = jnp.take(ext_table[face_idx ^ 1], lookup[face_idx], axis=-1)
        ghost_sets.append(jnp.where(neighbour_ids[face_idx] >= 0, picked, own_faces[face_idx]))
    return ghost_sets


def framed(inner_cells, side_cells):
    edge_cells = inner_cells.shape[0]
    block_count = inner_cells.shape[-1]
    framed_cells = jnp.zeros(
        (edge_cells + 2, edge_cells + 2, edge_cells + 2, block_count), inner_cells.dtype
    )
    framed_cells = framed_cells.at[1:-1, 1:-1, 1:-1].set(inner_cells)
    framed_cells = (
        framed_cells.at[0, 1:-1, 1:-1].set(side_cells[0]).at[-1, 1:-1, 1:-1].set(side_cells[1])
    )
    framed_cells = (
        framed_cells.at[1:-1, 0, 1:-1].set(side_cells[2]).at[1:-1, -1, 1:-1].set(side_cells[3])
    )
    framed_cells = (
        framed_cells.at[1:-1, 1:-1, 0].set(side_cells[4]).at[1:-1, 1:-1, -1].set(side_cells[5])
    )
    return framed_cells


def laplace(framed_cells, level_scale):
    centre = framed_cells[1:-1, 1:-1, 1:-1]
    beside_all = framed_cells[2:, 1:-1, 1:-1] + framed_cells[:-2, 1:-1, 1:-1]
    beside_all = beside_all + framed_cells[1:-1, 2:, 1:-1] + framed_cells[1:-1, :-2, 1:-1]
    beside_all = beside_all + framed_cells[1:-1, 1:-1, 2:] + framed_cells[1:-1, 1:-1, :-2]
    return level_scale * (beside_all - 6.0 * centre)


def slab_laplace(slab_cells, outer_layer, inner_layer, level_scale):
    padded = jnp.pad(slab_cells, ((1, 1), (1, 1), (0, 0)), mode="edge")
    tangent = (
        padded[2:, 1:-1]
        + padded[:-2, 1:-1]
        + padded[1:-1, 2:]
        + padded[1:-1, :-2]
        - 4.0 * slab_cells
    )
    return level_scale * (outer_layer + inner_layer - 2.0 * slab_cells + tangent)


def substep(current, ghost_sets, level_scale):
    order_field = current[0]
    surf_field = current[1]
    last_cell = order_field.shape[0] - 1
    inner_faces = [
        order_field[0],
        order_field[last_cell],
        order_field[:, 0],
        order_field[:, last_cell],
        order_field[:, :, 0],
        order_field[:, :, last_cell],
    ]
    order_sides = [ghost_set[0] for ghost_set in ghost_sets]
    order_lap = laplace(framed(order_field, order_sides), level_scale)
    potential = (
        order_field * order_field * order_field
        - order_field
        - STIFFNESS * order_lap
        - COUPLING * surf_field
    )
    side_potential = []
    for face_idx in range(6):
        slab_cells = ghost_sets[face_idx][0]
        side_lap = slab_laplace(
            slab_cells, ghost_sets[face_idx][1], inner_faces[face_idx], level_scale
        )
        side_potential.append(
            slab_cells * slab_cells * slab_cells
            - slab_cells
            - STIFFNESS * side_lap
            - COUPLING * ghost_sets[face_idx][2]
        )
    potential_lap = laplace(framed(potential, side_potential), level_scale)
    surf_excess = surf_field - SEGREGATE * order_field * order_field
    side_excess = [
        ghost_set[2] - SEGREGATE * ghost_set[0] * ghost_set[0] for ghost_set in ghost_sets
    ]
    excess_lap = laplace(framed(surf_excess, side_excess), level_scale)
    return jnp.stack(
        [order_field + MOBILITY_STEP * potential_lap, surf_field + DIFFUSE_STEP * excess_lap]
    )


def add_ints(left_val, right_val):
    return left_val + right_val


def neighbour_faces(face_data, first_live, end_live, reach_cap):
    head_part = lax.dynamic_slice_in_dim(face_data, first_live, reach_cap, 4)
    tail_part = lax.dynamic_slice_in_dim(face_data, end_live - reach_cap, reach_cap, 4)
    outer_faces = with_halo(jnp.concatenate([head_part, tail_part], 4), (("curve", 4),), reach_cap)
    return jnp.concatenate(
        [outer_faces[..., :reach_cap], face_data, outer_faces[..., 3 * reach_cap :]], 4
    )


def body(fields, weights, levels, neighbours):
    my_rank = lax.axis_index("curve")
    rank_count = lax.axis_size("curve")
    per_dev = weights.shape[0]
    move_cap = per_dev // 2
    reach_cap = per_dev // 4
    slot_count = per_dev + 2 * move_cap
    edge_cells = fields.shape[1]
    local_sum = jnp.sum(weights)
    before = prefix(local_sum, "curve", add_ints, jnp.int32(0))
    grand = lax.psum(local_sum.astype(jnp.float32), "curve").astype(jnp.int32)
    prior_weight = (before + jnp.cumsum(weights) - weights).astype(jnp.int32)
    new_owner = jnp.minimum(rank_count - 1, rank_count * prior_weight // grand)
    block_info = jnp.concatenate([levels[None, :], neighbours, (new_owner + 1)[None, :]], 0).astype(
        jnp.float32
    )
    flat_fields = fields.reshape(2 * edge_cells**3, per_dev)
    arrived, arrived_info = (
        with_halo(flat_fields, (("curve", 1),), move_cap),
        with_halo(block_info, (("curve", 1),), move_cap),
    )
    current = arrived.reshape(2, edge_cells, edge_cells, edge_cells, slot_count)
    level_scale = 1.0 + 3.0 * arrived_info[0]
    new_neighbours = arrived_info[1:7].astype(jnp.int32)
    slot_owner = arrived_info[7].astype(jnp.int32) - 1
    live_slot = slot_owner == my_rank
    from_left = jnp.sum(live_slot[:move_cap].astype(jnp.int32))
    from_right = jnp.sum(live_slot[move_cap + per_dev :].astype(jnp.int32))
    gone_left = jnp.sum((new_owner < my_rank).astype(jnp.int32))
    gone_right = jnp.sum((new_owner > my_rank).astype(jnp.int32))
    first_live = move_cap - from_left + gone_left
    end_live = move_cap + per_dev - gone_right + from_right
    base_id = my_rank * per_dev
    low_id = base_id - move_cap + first_live
    high_id = base_id - move_cap + end_live
    near_lookup = jnp.where(
        new_neighbours < low_id,
        new_neighbours - low_id + reach_cap,
        jnp.where(
            new_neighbours >= high_id,
            reach_cap + slot_count + new_neighbours - high_id,
            reach_cap + new_neighbours - base_id + move_cap,
        ),
    )
    near_lookup = jnp.clip(near_lookup, 0, slot_count + 2 * reach_cap - 1)
    for step_idx in range(2):
        face_data = face_table(current)
        extended = neighbour_faces(face_data, first_live, end_live, reach_cap)
        ghost_sets = ghosts(extended, near_lookup, new_neighbours, face_data)
        current = substep(current, ghost_sets, level_scale)
    return current * live_slot.astype(jnp.float32)


def solution(mesh):
    in_specs = (P(None, None, None, None, "curve"), P("curve"), P("curve"), P(None, "curve"))
    out_specs = P(None, None, None, None, "curve")
    return jax.shard_map(body, mesh=mesh, in_specs=in_specs, out_specs=out_specs, check_vma=False)
```

profile of v0, /device:TPU:6, one launch (start us, length us, event | category | flops | bytes accessed | tf_op | source)
XLA Modules:
  0.0 801.8 jit_solution(3577997176880901525)
XLA Ops:
  2.7 65.9 %all-reduce.6 = s32[128]{0:T(128)S(1)} all-reduce(s32[128]{0:T(128)S(1)} %dynamic-update-slice.126), channel_id=1, replica_groups=mesh['curve'=128] {'curve'}, use_global_device_ids=true, to_apply=%add.6 | all-reduce | flops 128 | bytes 1024
  68.6 161.0 %while.55 = (s32[]{:T(128)}, s32[]{:T(128)}, s32[]{:T(128)}, s32[128]{0:T(128)S(1)}, s32[]{:T(128)}) while((s32[]{:T(128)}, s32[]{:T(128)}, s32[]{:T(128)}, s32[128]{0:T(128)S(1)}, s32[]{:T(128)}) %tuple.296), condition=%wide.region_2.3_spmd, body=%wide.region_1.2_spmd.sunk | while | flops 5 | bytes 107 | solution.py:40
  230.5 64.4 %psum.7 = f32[]{:T(128)} all-reduce(f32[]{:T(128)S(6)} %convert_element_type.44), channel_id=1, replica_groups=mesh['curve'=128] {'curve'}, use_global_device_ids=true, to_apply=%region_4.5 | all-reduce | flops 1 | bytes 8 | tf_op jit(solution)/shard_map/psum | solution.py:180
  299.8 7.9 collective-permute-start.3
  307.7 8.0 %fusion.259 = (f32[8192,32]{1,0:T(8,128)}, f32[8192,32]{1,0:T(8,128)}) fusion(f32[8192,64]{1,0:T(8,128)} %bitcast.511), kind=kLoop, calls=%fused_computation.607 | loop fusion | bytes 4194304 | tf_op jit(solution)/shard_map/slice | solution.py:18
  323.2 7.9 collective-permute-start.1
  343.4 3.7 copy.2464
  360.3 8.5 %collective-permute-start.5 = (f32[6,3,16,16,16]{4,3,2,1,0:T(8,128)S(1)}, f32[6,3,16,16,16]{4,3,2,1,0:T(8,128)S(1)}, u32[]{:S(2)}, u32[]{:S(2)}) collective-permute-start(f32[6,3,16,16,16]{4,3,2,1,0:T(8,128)S(1)} %get-tuple-element.647), channel_id=1, source_target_pairs={{1,0},{2,1},{3,2},{4,3},{5,4},{6,5},{7,6},{8,7},{9,8},{10,9},{11,1... | collective-permute-start | bytes 884744 | tf_op jit(solution)/shard_map/ppermute | solution.py:23
  372.3 20.8 %collective-permute-done.4 = f32[6,3,16,16,16]{4,3,2,1,0:T(8,128)S(1)} collective-permute-done((f32[6,3,16,16,16]{4,3,2,1,0:T(8,128)S(1)}, f32[6,3,16,16,16]{4,3,2,1,0:T(8,128)S(1)}, u32[]{:S(2)}, u32[]{:S(2)}) %collective-permute-start.4) | collective-permute-done | bytes 294944 | tf_op jit(solution)/shard_map/ppermute | solution.py:21
  399.0 3.5 copy.2550
  402.5 4.7 gather_fusion.4
  410.3 3.5 copy.2551
  413.8 4.7 gather_fusion.5
  428.2 4.6 gather_fusion.2
  435.8 3.5 copy.2549
  439.3 4.7 gather_fusion.3
  456.0 3.5 copy.2546
  459.5 4.6 gather_fusion
  469.7 4.7 gather_fusion.1
  488.4 4.5 scatter.149
  492.9 4.5 scatter.150
  497.4 10.2 %fusion.4 = (f32[16,16,16,128]{3,2,1,0:T(8,128)S(1)}, f32[16,16,16,128]{3,2,1,0:T(8,128)S(1)}) fusion(f32[16,16,16,128]{3,2,1,0:T(8,128)} %bitcast.523, f32[16,16,16,128]{3,2,1,0:T(8,128)S(1)} %bitcast.517, f32[18,18,18,128]{3,2,1,0:T(8,128)} %scatter.150, f32[128]{0:T(128)S(1)} %add_bitcast_fusion), kind=kLoop, calls=%fused_computation.24 | loop fusion | flops 8912896 | bytes 23069184 | tf_op jit(solution)/shard_map/sub | solution.py:147
  520.7 4.6 scatter.174
  525.3 4.7 scatter.175
  546.3 4.5 scatter.160
  551.6 4.5 scatter.161
  556.1 20.4 %fusion.5 = (f32[16,16,16,128]{3,2,1,0:T(8,128)}, f32[16,16,16,128]{3,2,1,0:T(8,128)S(1)}, f32[16,16,16,128]{3,2,1,0:T(8,128)}) fusion(f32[16,16,16,128]{3,2,1,0:T(8,128)} %bitcast.520, f32[18,18,18,128]{3,2,1,0:T(8,128)} %scatter.161, f32[128]{0:T(128)S(1)} %add_bitcast_fusion, f32[16,16,16,128]{3,2,1,0:T(8,128)} %bitcast.524, f32[18,18,18,128]{3,2,1,0:T(8,128)} %scatter.175), kind=kLoop, calls=%fused_computation.25 | loop fusion | flops 12058624 | bytes 39846400 | tf_op jit(solution)/shard_map/sub | solution.py:147
  585.3 8.2 %collective-permute-start.7 = (f32[6,3,16,16,16]{4,3,2,1,0:T(8,128)S(1)}, f32[6,3,16,16,16]{4,3,2,1,0:T(8,128)S(1)}, u32[]{:S(2)}, u32[]{:S(2)}) collective-permute-start(f32[6,3,16,16,16]{4,3,2,1,0:T(8,128)S(1)} %get-tuple-element.645), channel_id=1, source_target_pairs={{1,0},{2,1},{3,2},{4,3},{5,4},{6,5},{7,6},{8,7},{9,8},{10,9},{11,1... | collective-permute-start | bytes 884744 | tf_op jit(solution)/shard_map/ppermute | solution.py:23
  598.0 19.9 %collective-permute-done.6 = f32[6,3,16,16,16]{4,3,2,1,0:T(8,128)S(1)} collective-permute-done((f32[6,3,16,16,16]{4,3,2,1,0:T(8,128)S(1)}, f32[6,3,16,16,16]{4,3,2,1,0:T(8,128)S(1)}, u32[]{:S(2)}, u32[]{:S(2)}) %collective-permute-start.6) | collective-permute-done | bytes 294944 | tf_op jit(solution)/shard_map/ppermute | solution.py:21
  623.7 3.8 copy.2560
  627.4 4.6 gather_fusion.11
  637.6 3.6 copy.2559
  641.2 4.6 gather_fusion.10
  651.5 3.6 copy.2558
  655.1 4.6 gather_fusion.9
  665.4 3.6 copy.2557
  669.0 4.6 gather_fusion.8
  679.3 3.6 copy.2556
  682.8 4.6 gather_fusion.7
  695.8 4.5 gather_fusion.6
  716.5 4.6 scatter.206
  721.1 4.5 scatter.209
  732.3 4.5 scatter.184
  736.8 4.5 scatter.185
  741.3 20.0 %fusion.3 = (f32[16,16,16,128]{3,2,1,0:T(8,128)S(1)}, f32[1,16,16,16,128]{4,3,2,1,0:T(8,128)}) fusion(f32[16,16,16,128]{3,2,1,0:T(8,128)S(1)} %get-tuple-element.605, f32[18,18,18,128]{3,2,1,0:T(8,128)} %scatter.185, f32[16,16,16,128]{3,2,1,0:T(8,128)} %get-tuple-element.606, f32[128]{0:T(128)S(1)} %add_bitcast_fusion, f32[18,18,18,128]{3,2,1,0:T(8,128)} %scatter.209), kind=kLoop, calls=%fused_computation.23 | loop fusion | flops 12582912 | bytes 37749248 | tf_op jit(solution)/shard_map/sub | solution.py:129
  778.8 4.5 scatter.195
  784.7 4.5 scatter.196
  789.2 9.5 %fusion.15 = f32[1,16,16,16,128]{4,3,2,1,0:T(8,128)S(1)} fusion(f32[16,16,16,128]{3,2,1,0:T(8,128)S(1)} %get-tuple-element.605, f32[18,18,18,128]{3,2,1,0:T(8,128)} %scatter.196, f32[128]{0:T(128)S(1)} %add_bitcast_fusion), kind=kLoop, calls=%fused_computation.42 | loop fusion | flops 5242880 | bytes 18874880 | tf_op jit(solution)/shard_map/stack | solution.py:152
  (441 shorter events, 293.2 us)
Async XLA Ops:
  297.9 33.8 %collective-permute-start.2 = (f32[8,32]{1,0:T(8,128)S(1)}, f32[8,32]{1,0:T(8,128)S(1)}, u32[]{:S(2)}, u32[]{:S(2)}) collective-permute-start(f32[8,32]{1,0:T(8,128)S(1)} %get-tuple-element.747), channel_id=1, source_target_pairs={{0,1},{1,2},{2,3},{3,4},{4,5},{5,6},{6,7},{7,8},{8,9},{9,10},{10,1... | collective-permute-start | bytes 3080 | tf_op jit(solution)/shard_map/ppermute | solution.py:21
  299.8 31.9 %collective-permute-start.3 = (f32[8,32]{1,0:T(8,128)S(1)}, f32[8,32]{1,0:T(8,128)S(1)}, u32[]{:S(2)}, u32[]{:S(2)}) collective-permute-start(f32[8,32]{1,0:T(8,128)S(1)} %get-tuple-element.748), channel_id=1, source_target_pairs={{1,0},{2,1},{3,2},{4,3},{5,4},{6,5},{7,6},{8,7},{9,8},{10,9},{11,1... | collective-permute-start | bytes 3080 | tf_op jit(solution)/shard_map/ppermute | solution.py:23
  318.5 20.3 %collective-permute-start = (f32[8192,32]{0,1:T(8,128)S(1)}, f32[8192,32]{0,1:T(8,128)S(1)}, u32[]{:S(2)}, u32[]{:S(2)}) collective-permute-start(f32[8192,32]{0,1:T(8,128)S(1)} %copy.2461), channel_id=1, source_target_pairs={{0,1},{1,2},{2,3},{3,4},{4,5},{5,6},{6,7},{7,8},{8,9},{9,10},{10,1... | collective-permute-start | bytes 3145736 | tf_op jit(solution)/shard_map/ppermute | solution.py:21
  323.2 20.2 %collective-permute-start.1 = (f32[8192,32]{0,1:T(8,128)S(1)}, f32[8192,32]{0,1:T(8,128)}, u32[]{:S(2)}, u32[]{:S(2)}) collective-permute-start(f32[8192,32]{0,1:T(8,128)S(1)} %copy.2462), channel_id=1, source_target_pairs={{1,0},{2,1},{3,2},{4,3},{5,4},{6,5},{7,6},{8,7},{9,8},{10,9},{11,1... | collective-permute-start | bytes 3145736 | tf_op jit(solution)/shard_map/ppermute | solution.py:23
  336.6 91.5 %copy-start.64 = (s32[1024]{0:T(1024)}, s32[1024]{0:T(1024)S(1)}, u32[]{:S(2)}) copy-start(s32[1024]{0:T(1024)S(1)} %pad_clamp_fusion.3) | copy-start | bytes 12292
  347.1 3.0 copy-start
  347.1 4.3 copy-start.2
  347.1 5.5 copy-start.3
  352.5 3.3 copy-start.31
  352.5 3.3 copy-start.32
  352.5 3.4 copy-start.29
  352.5 3.4 copy-start.30
  355.0 186.7 %copy-start.1 = (f32[4096,128]{1,0:T(8,128)}, f32[4096,128]{1,0:T(8,128)S(1)}, u32[]{:S(2)}) copy-start(f32[4096,128]{1,0:T(8,128)S(1)} %get-tuple-element.641) | copy-start | bytes 6291460
  357.1 11.7 %copy-start.71 = (s32[128]{0:T(128)S(1)}, s32[128]{0:T(128)}, u32[]{:S(2)}) copy-start(s32[128]{0:T(128)} %get-tuple-element.744) | copy-start | bytes 1540
  358.4 34.7 %collective-permute-start.4 = (f32[6,3,16,16,16]{4,3,2,1,0:T(8,128)S(1)}, f32[6,3,16,16,16]{4,3,2,1,0:T(8,128)S(1)}, u32[]{:S(2)}, u32[]{:S(2)}) collective-permute-start(f32[6,3,16,16,16]{4,3,2,1,0:T(8,128)S(1)} %get-tuple-element.646), channel_id=1, source_target_pairs={{0,1},{1,2},{2,3},{3,4},{4,5},{5,6},{6,7},{7,8},{8,9},{9,10},{10,1... | collective-permute-start | bytes 884744 | tf_op jit(solution)/shard_map/ppermute | solution.py:21
  360.3 34.8 %collective-permute-start.5 = (f32[6,3,16,16,16]{4,3,2,1,0:T(8,128)S(1)}, f32[6,3,16,16,16]{4,3,2,1,0:T(8,128)S(1)}, u32[]{:S(2)}, u32[]{:S(2)}) collective-permute-start(f32[6,3,16,16,16]{4,3,2,1,0:T(8,128)S(1)} %get-tuple-element.647), channel_id=1, source_target_pairs={{1,0},{2,1},{3,2},{4,3},{5,4},{6,5},{7,6},{8,7},{9,8},{10,9},{11,1... | collective-permute-start | bytes 884744 | tf_op jit(solution)/shard_map/ppermute | solution.py:23
  413.8 7.7 copy-start.67
  439.3 7.7 copy-start.65
  439.3 7.7 copy-start.66
  448.6 6.2 copy-start.12
  448.6 6.8 copy-start.14
  478.8 28.8 %copy-start.20 = (f32[3,16,16,128]{3,2,1,0:T(8,128)}, f32[3,16,16,128]{3,2,1,0:T(8,128)S(1)}, u32[]{:S(2)}) copy-start(f32[3,16,16,128]{3,2,1,0:T(8,128)S(1)} %get-tuple-element.753) | copy-start | bytes 1179652
  478.8 28.8 %copy-start.21 = (f32[3,16,16,128]{3,2,1,0:T(8,128)}, f32[3,16,16,128]{3,2,1,0:T(8,128)S(1)}, u32[]{:S(2)}) copy-start(f32[3,16,16,128]{3,2,1,0:T(8,128)S(1)} %get-tuple-element.754) | copy-start | bytes 1179652
  512.2 25.6 %copy-start.15 = (f32[3,16,16,128]{3,2,1,0:T(8,128)S(1)}, f32[3,16,16,128]{3,2,1,0:T(8,128)}, u32[]{:S(2)}) copy-start(f32[3,16,16,128]{3,2,1,0:T(8,128)} %copy-done.14) | copy-start | bytes 1179652
  513.9 27.9 %copy-start.13 = (f32[3,16,16,128]{3,2,1,0:T(8,128)S(1)}, f32[3,16,16,128]{3,2,1,0:T(8,128)}, u32[]{:S(2)}) copy-start(f32[3,16,16,128]{3,2,1,0:T(8,128)} %copy-done.12) | copy-start | bytes 1179652
  532.1 18.7 %copy-start.27 = (f32[16,16,1,128]{3,2,1,0:T(1,128)S(1)}, f32[16,16,1,128]{3,2,1,0:T(1,128)}, u32[]{:S(2)}) copy-start(f32[16,16,1,128]{3,2,1,0:T(1,128)} %copy-done.26) | copy-start | bytes 393220
  536.0 14.8 %copy-start.60 = (f32[16,16,128]{2,1,0:T(8,128)S(1)}, f32[16,16,128]{2,1,0:T(8,128)}, u32[]{:S(2)}) copy-start(f32[16,16,128]{2,1,0:T(8,128)} %get-tuple-element.713) | copy-start | bytes 393220
  576.6 4.8 copy-start.34
  576.6 4.8 copy-start.35
  576.7 4.8 copy-start.41
  576.7 4.8 copy-start.42
  576.7 4.8 copy-start.43
  576.7 4.8 copy-start.44
  577.9 3.7 copy-start.33
  577.9 3.7 copy-start.36
  583.4 34.5 %collective-permute-start.6 = (f32[6,3,16,16,16]{4,3,2,1,0:T(8,128)S(1)}, f32[6,3,16,16,16]{4,3,2,1,0:T(8,128)S(1)}, u32[]{:S(2)}, u32[]{:S(2)}) collective-permute-start(f32[6,3,16,16,16]{4,3,2,1,0:T(8,128)S(1)} %get-tuple-element.644), channel_id=1, source_target_pairs={{0,1},{1,2},{2,3},{3,4},{4,5},{5,6},{6,7},{7,8},{8,9},{9,10},{10,1... | collective-permute-start | bytes 884744 | tf_op jit(solution)/shard_map/ppermute | solution.py:21
  585.3 10.4 %copy-start.6 = (f32[16,16,16,128]{3,2,1,0:T(8,128)S(1)}, f32[16,16,16,128]{3,2,1,0:T(8,128)}, u32[]{:S(2)}) copy-start(f32[16,16,16,128]{3,2,1,0:T(8,128)} %get-tuple-element.604) | copy-start | bytes 6291460
  585.3 34.5 %collective-permute-start.7 = (f32[6,3,16,16,16]{4,3,2,1,0:T(8,128)S(1)}, f32[6,3,16,16,16]{4,3,2,1,0:T(8,128)S(1)}, u32[]{:S(2)}, u32[]{:S(2)}) collective-permute-start(f32[6,3,16,16,16]{4,3,2,1,0:T(8,128)S(1)} %get-tuple-element.645), channel_id=1, source_target_pairs={{1,0},{2,1},{3,2},{4,3},{5,4},{6,5},{7,6},{8,7},{9,8},{10,9},{11,1... | collective-permute-start | bytes 884744 | tf_op jit(solution)/shard_map/ppermute | solution.py:23
  627.4 7.7 copy-start.68
  627.4 7.7 copy-start.69
  700.4 7.4 copy-start.10
  700.4 8.0 copy-start.8
  704.6 27.8 %copy-start.58 = (f32[1,16,16,128]{3,2,1,0:T(8,128)S(1)}, f32[1,16,16,128]{3,2,1,0:T(8,128)}, u32[]{:S(2)}) copy-start(f32[1,16,16,128]{3,2,1,0:T(8,128)} %get-tuple-element.683) | copy-start | bytes 393220
  705.5 31.4 %copy-start.57 = (f32[1,16,16,128]{3,2,1,0:T(8,128)S(1)}, f32[1,16,16,128]{3,2,1,0:T(8,128)}, u32[]{:S(2)}) copy-start(f32[1,16,16,128]{3,2,1,0:T(8,128)} %get-tuple-element.679) | copy-start | bytes 393220
  763.6 13.8 %copy-start.25 = (f32[16,16,1,128]{3,2,1,0:T(1,128)S(1)}, f32[16,16,1,128]{3,2,1,0:T(1,128)}, u32[]{:S(2)}) copy-start(f32[16,16,1,128]{3,2,1,0:T(1,128)} %copy-done.24) | copy-start | bytes 393220
  763.6 19.7 %copy-start.23 = (f32[16,16,1,128]{3,2,1,0:T(1,128)S(1)}, f32[16,16,1,128]{3,2,1,0:T(1,128)}, u32[]{:S(2)}) copy-start(f32[16,16,1,128]{3,2,1,0:T(1,128)} %copy-done.22) | copy-start | bytes 393220
  789.2 9.5 %copy-start.5 = (f32[1,16,16,16,128]{4,3,2,1,0:T(8,128)S(1)}, f32[1,16,16,16,128]{4,3,2,1,0:T(8,128)}, u32[]{:S(2)}) copy-start(f32[1,16,16,16,128]{4,3,2,1,0:T(8,128)} %get-tuple-element.649) | copy-start | bytes 6291460
  789.2 9.5 %copy-start.70 = (f32[128]{0:T(128)S(1)}, f32[128]{0:T(128)}, u32[]{:S(2)}) copy-start(f32[128]{0:T(128)} %get-tuple-element.602) | copy-start | bytes 1540
  (32 other events, 49.8 us)
where the time goes:
time: 817 us; the launch traced here: 802 us
  local copies, waits for them, and re-layouts  369 us (45%)
  blocking collectives  130 us (16%)
  other arithmetic  123 us (15%)
  loops' own time  85.9 us (11%)
  waiting for transfers between devices  48.1 us (6%)
  starting transfers between devices  40 us (5%)
    gather x24, local copies, waits for them, and re-layouts, ghosts(): picked = jnp.take(ext_table[face_idx ^ 1], lookup[face_idx], axis=-1)  91.8 us
    another operation x1, loops' own time, prefix(): return lax.fori_loop(0, peers, step, start)  85.9 us
    dynamic_slice x128, local copies, waits for them, and re-layouts, step(): new = combine(before, everything[k])  75 us
    unnamed x1, blocking collectives  65.9 us
    psum x1, blocking collectives, body(): grand = lax.psum(local_sum.astype(jnp.float32), 'curve').astype(jnp.int32)  64.4 us
    scatter x12, local copies, waits for them, and re-layouts, framed(): framed_cells.at[1:-1, 1:-1, 0].set(side_cells[4]).at[1:-1, 1:-1, -1]  54.3 us
    unnamed x158, local copies, waits for them, and re-layouts  46.9 us
    ppermute x4, waiting for transfers between devices, with_halo(): lax.ppermute(tail, axis, [(i, (i + 1) % count) for i in range(ends)])  42.2 us
  transfers between devices with their start and end apart: 8, of which 6 were waited for; matrix products, arithmetic and copies ran while one was open for 3% of the time, Pallas kernels for 0%

commit v1 on v0

v1 whole, which is shorter than its diff:
```python
import jax
import jax.numpy as jnp
from jax import lax
from jax.experimental import pallas as pl
from jax.experimental.pallas import tpu as pltpu
from jax.sharding import PartitionSpec as P

MOBILITY_STEP = 0.0006
DIFFUSE_STEP = 0.01
BS = 16
PER = 64
STAGES = ((1, 8), (8, 4), (32, 4))
PARTNERS = sum(size - 1 for _, size in STAGES)
PLANES = 2
CHUNKS = BS // PLANES
ORDER = (0, 1, 2, 3, 4, 5)
Z0 = 8
Z1 = Z0 + BS
MESH = pl.DeviceIdType.MESH
F32 = jnp.float32


def kernel(
    fields, weights, levels, nbrs, out,
    raw, wraw, lraw, nraw,
    cp, mp, ep, sf, ftz, slab, slab2, ints, kap, wown, wleft, wright, st0, st1, st2,
    spk, rpk, spk3, rpk3,
    in_sem, face_send, face_recv, move_send, move_recv, sum_send, sum_recv, w_send, w_recv,
):
    me = lax.axis_index("curve")
    count = lax.axis_size("curve")
    right = lax.rem(me + 1, count)
    left = lax.rem(me + count - 1, count)
    stage_bufs = (st0, st1, st2)

    def partner(stage, j):
        stride, size = STAGES[stage]
        digit = lax.rem(me // stride, size)
        return me + (lax.rem(digit + j, size) - digit) * stride

    loads = [
        pltpu.make_async_copy(fields.at[0], raw.at[0], in_sem.at[0]),
        pltpu.make_async_copy(fields.at[1], raw.at[1], in_sem.at[1]),
        pltpu.make_async_copy(weights, wraw, in_sem.at[2]),
        pltpu.make_async_copy(levels, lraw, in_sem.at[3]),
        pltpu.make_async_copy(nbrs, nraw, in_sem.at[4]),
    ]
    for load in loads:
        load.start()

    barrier = pltpu.get_barrier_semaphore()
    for peer in (left, right):
        pl.semaphore_signal(barrier, inc=1, device_id=(peer,), device_id_type=MESH)
    for stage, (_, size) in enumerate(STAGES):
        for j in range(1, size):
            pl.semaphore_signal(barrier, inc=1, device_id=(partner(stage, j),), device_id_type=MESH)

    lane = lax.broadcasted_iota(jnp.int32, (BS, 128), 1)
    slot16 = lane // 16
    slot32 = lane // 32

    blank = jnp.zeros((BS, 128), F32)
    for a in range(BS):
        cp[0, 1 + a, Z0:Z1] = blank
        cp[BS + 1, 1 + a, Z0:Z1] = blank
        cp[1 + a, 0, Z0:Z1] = blank
        cp[1 + a, BS + 1, Z0:Z1] = blank
        cp[1 + a, 1 : BS + 1, Z0 - 1] = blank
        cp[1 + a, 1 : BS + 1, Z1] = blank

    ints[...] = jnp.zeros((8, 128), jnp.int32)
    kap[...] = jnp.zeros((8, 128), F32)
    wown[...] = jnp.zeros((8, 128), F32)
    for load in loads[2:]:
        load.wait()
    ints[0:6, 0:PER] = nraw[...]
    kap[0:1, 0:PER] = 1.0 + 3.0 * lraw[...].astype(F32)
    wown[0:1, 0:PER] = wraw[...].astype(F32)
    kappa = jnp.broadcast_to(kap[0:1], (BS, 128))
    st0[0:1] = jnp.broadcast_to(jnp.sum(wown[0:1], axis=1, keepdims=True), (1, 128))

    loads[0].wait()

    @pl.loop(0, BS)
    def _(x):
        for y in range(BS):
            cp[x + 1, y + 1, Z0:Z1, 0:PER] = raw[0, x, y]

    loads[1].wait()

    @pl.loop(0, BS)
    def _(x):
        for y in range(BS):
            sf[x, y, :, 0:PER] = raw[1, x, y]

    pl.semaphore_wait(barrier, 2 + PARTNERS)

    copies = []

    def send(src, dst, send_sem, recv_sem, peer):
        copy = pltpu.make_async_remote_copy(
            src_ref=src, dst_ref=dst, send_sem=send_sem, recv_sem=recv_sem,
            device_id=(peer,), device_id_type=MESH,
        )
        copy.start()
        copies.append(copy)
        return copy

    def send_sums(stage):
        buf = stage_bufs[stage]
        base = sum(size - 1 for _, size in STAGES[:stage]) - 1
        return [
            send(buf.at[pl.ds(0, 1)], buf.at[pl.ds(j, 1)], sum_send.at[base + j], sum_recv.at[base + j], partner(stage, j))
            for j in range(1, STAGES[stage][1])
        ]

    def take_sums(stage, arrivals):
        for copy in arrivals:
            copy.wait_recv()
        stride, size = STAGES[stage]
        digit = lax.rem(me // stride, size)
        row = lax.broadcasted_iota(jnp.int32, (8, 128), 0)
        values = stage_bufs[stage][...]
        before = jnp.sum(jnp.where((row >= 1) & (row <= digit), values, 0.0), axis=0, keepdims=True)
        whole = jnp.sum(jnp.where(row < size, values, 0.0), axis=0, keepdims=True)
        return before, whole

    def own(f, layer, a):
        if f >= 4:
            return ftz[f - 4, layer, a]
        depth = 1 if layer == 1 else 0
        at = depth if f % 2 == 0 else BS - 1 - depth
        if f < 2:
            return sf[at, a] if layer == 2 else cp[1 + at, 1 + a, Z0:Z1]
        return sf[a, at] if layer == 2 else cp[1 + a, 1 + at, Z0:Z1]

    def draw_z():
        for a in range(BS):
            ftz[0, 0, a] = cp[1 + a, 1 : BS + 1, Z0]
            ftz[0, 1, a] = cp[1 + a, 1 : BS + 1, Z0 + 1]
            ftz[0, 2, a] = sf[a, :, 0]
            ftz[1, 0, a] = cp[1 + a, 1 : BS + 1, Z1 - 1]
            ftz[1, 1, a] = cp[1 + a, 1 : BS + 1, Z1 - 2]
            ftz[1, 2, a] = sf[a, :, BS - 1]

    def pack_face(step, f):
        for layer in range(3):
            for aa in range(2):
                to_left = to_right = None
                for j in range(8):
                    rows = own(f, layer, 2 * j + aa)
                    turned = pltpu.roll(rows, 16 * j, axis=1) if j else rows
                    to_left = turned if j == 0 else jnp.where(slot16 == j, turned, to_left)
                    to_right = turned if j == 0 else jnp.where(slot16 == (j + 3) % 8, turned, to_right)
                spk[step, 0, f, layer, aa] = to_left
                spk[step, 1, f, layer, aa] = to_right
        return [
            send(spk.at[step, d, f], rpk.at[step, d, f], face_send.at[step, d, f], face_recv.at[step, d, f], peer)
            for d, peer in ((0, left), (1, right))
        ]

    def ghost_face(step, f, arrivals):
        g = f ^ 1
        for copy in arrivals:
            copy.wait_recv()
        lookup = jnp.broadcast_to(ints[f : f + 1], (BS, 128))
        inside = lookup >= 0
        lookup = jnp.bitwise_and(lookup - me * PER, 127)
        for layer in range(3):
            for aa in range(2):
                from_right = rpk[step, 0, g, layer, aa]
                from_left = rpk[step, 1, g, layer, aa]
                for j in range(8):
                    a = 2 * j + aa
                    both = jnp.where(slot16 == (j + 3) % 8, from_left, from_right)
                    shift = (16 * (4 - j)) % 128
                    halo = pltpu.roll(both, shift, axis=1) if shift else both
                    table = jnp.where(lane < PER, own(g, layer, a), halo)
                    picked = jnp.take_along_axis(table, lookup, axis=1, mode="promise_in_bounds")
                    ghost = jnp.where(inside, picked, own(f, layer, a))
                    if layer == 0:
                        slab[f, a, Z0:Z1] = ghost
                        slab[f, a, Z0 - 1 : Z0] = ghost[0:1]
                        slab[f, a, Z1 : Z1 + 1] = ghost[BS - 1 : BS]
                    else:
                        slab2[f, layer - 1, a] = ghost
        for a in range(BS):
            g1 = slab[f, a, Z0:Z1]
            g2 = slab2[f, 0, a]
            gs = slab2[f, 1, a]
            around = slab[f, max(a - 1, 0), Z0:Z1] + slab[f, min(a + 1, BS - 1), Z0:Z1]
            around = around + slab[f, a, Z0 - 1 : Z1 - 1] + slab[f, a, Z0 + 1 : Z1 + 1]
            lap = kappa * (g2 + own(f, 0, a) + around - 6.0 * g1)
            square = g1 * g1
            mu = g1 * square - g1 - lap - 0.5 * gs
            excess = gs - 0.5 * square
            part = kappa * g1
            if f < 2:
                edge = 0 if f == 0 else BS + 1
                cell = 1 if f == 0 else BS
                mp[edge, 1 + a, Z0:Z1] = mu
                ep[edge, 1 + a, Z0:Z1] = excess
                mp[cell, 1 + a, Z0:Z1] = mp[cell, 1 + a, Z0:Z1] - part
            elif f < 4:
                edge = 0 if f == 2 else BS + 1
                cell = 1 if f == 2 else BS
                mp[1 + a, edge, Z0:Z1] = mu
                ep[1 + a, edge, Z0:Z1] = excess
                mp[1 + a, cell, Z0:Z1] = mp[1 + a, cell, Z0:Z1] - part
            else:
                edge = Z0 - 1 if f == 4 else Z1
                cell = Z0 if f == 4 else Z1 - 1
                mp[1 + a, 1 : BS + 1, edge] = mu
                ep[1 + a, 1 : BS + 1, edge] = excess
                mp[1 + a, 1 : BS + 1, cell] = mp[1 + a, 1 : BS + 1, cell] - part

    def around_of(ref, x, y):
        total = ref[x, y + 1, Z0:Z1] + ref[x + 2, y + 1, Z0:Z1]
        total = total + ref[x + 1, y, Z0:Z1] + ref[x + 1, y + 2, Z0:Z1]
        return total + ref[x + 1, y + 1, Z0 - 1 : Z1 - 1] + ref[x + 1, y + 1, Z0 + 1 : Z1 + 1]

    def potentials():
        bias = 6.0 * kappa - 1.0

        @pl.loop(0, BS)
        def _(x):
            for y in range(BS):
                c = cp[x + 1, y + 1, Z0:Z1]
                s = sf[x, y]
                square = c * c
                mp[x + 1, y + 1, Z0:Z1] = c * (square + bias) - kappa * around_of(cp, x, y) - 0.5 * s
                ep[x + 1, y + 1, Z0:Z1] = s - 0.5 * square

    c_rate = MOBILITY_STEP * kappa
    s_rate = DIFFUSE_STEP * kappa

    def next_c(x, y):
        return cp[x + 1, y + 1, Z0:Z1] + c_rate * (around_of(mp, x, y) - 6.0 * mp[x + 1, y + 1, Z0:Z1])

    def next_s(x, y):
        return sf[x, y] + s_rate * (around_of(ep, x, y) - 6.0 * ep[x + 1, y + 1, Z0:Z1])

    def exchange_faces(step):
        draw_z()
        arrivals = {f: pack_face(step, f) for f in ORDER}
        if step == 0:
            sent["w"] = [
                send(wown.at[pl.ds(0, 1)], wright.at[pl.ds(0, 1)], w_send.at[0], w_recv.at[0], left),
                send(wown.at[pl.ds(0, 1)], wleft.at[pl.ds(0, 1)], w_send.at[1], w_recv.at[1], right),
            ]
            sent["sums"] = send_sums(0)
        potentials()
        for f in ORDER:
            ghost_face(step, f ^ 1, arrivals[f])

    sent = {}
    exchange_faces(0)

    before, whole = take_sums(0, sent["sums"])
    st1[0:1] = whole
    sums1 = send_sums(1)

    @pl.loop(0, BS)
    def _(x):
        for y in range(BS):
            cp[x + 1, y + 1, Z0:Z1] = next_c(x, y)
            sf[x, y] = next_s(x, y)

    before1, whole = take_sums(1, sums1)
    st2[0:1] = whole
    sums2 = send_sums(2)
    before = before + before1

    exchange_faces(1)

    turns = (0, 64, 32, 96)
    moves = []
    for chunk in range(CHUNKS):

        @pl.loop(chunk * PLANES, (chunk + 1) * PLANES)
        def _(x):
            for comp, update in ((0, next_c), (1, next_s)):
                for yy in range(4):
                    turned = []
                    for j in range(4):
                        value = update(x, 4 * j + yy)
                        out[comp, x, 4 * j + yy] = pltpu.roll(value, 32, axis=1)
                        turned.append(pltpu.roll(value, turns[j], axis=1) if turns[j] else value)
                    u0, u1, u2, u3 = turned
                    spk3[0, x, comp, yy] = jnp.where(slot32 == 0, u0, jnp.where(slot32 == 2, u1, jnp.where(slot32 == 1, u2, u3)))
                    spk3[1, x, comp, yy] = jnp.where(slot32 == 1, u0, jnp.where(slot32 == 3, u1, jnp.where(slot32 == 2, u2, u3)))

        planes = pl.ds(chunk * PLANES, PLANES)
        moves.append([
            send(spk3.at[d, planes], rpk3.at[d, planes], move_send.at[d, chunk], move_recv.at[d, chunk], peer)
            for d, peer in ((0, left), (1, right))
        ])

    before2, total = take_sums(2, sums2)
    before = before + before2
    for copy in sent["w"]:
        copy.wait_recv()
    lane1 = lax.broadcasted_iota(jnp.int32, (8, 128), 1)
    ours = jnp.broadcast_to(wown[0:1], (8, 128))
    lefts = jnp.broadcast_to(wleft[0:1], (8, 128))
    rights = jnp.broadcast_to(wright[0:1], (8, 128))
    window = jnp.where(
        (lane1 >= 32) & (lane1 < 96),
        pltpu.roll(ours, 32, axis=1),
        pltpu.roll(jnp.where(lane1 < 32, rights, lefts), 96, axis=1),
    )
    earlier = (lax.broadcasted_iota(jnp.int32, (128, 128), 0) < lax.broadcasted_iota(jnp.int32, (128, 128), 1)).astype(F32)
    upto = jnp.dot(window, earlier, preferred_element_type=F32)
    lead = jnp.sum(jnp.where(lane1 < 32, window, 0.0), axis=1, keepdims=True)
    prior = (jnp.broadcast_to(before, (8, 128)) - lead + upto).astype(jnp.int32) * count
    whole_sum = jnp.broadcast_to(total, (8, 128)).astype(jnp.int32)
    live8 = (prior >= me * whole_sum) & (prior < (me + 1) * whole_sum)
    live = jnp.broadcast_to(live8.astype(F32)[0:1], (BS, 128)) > 0.5

    odd = jnp.bitwise_and(slot32, 1) == 1
    middle = (lane >= 32) & (lane < 96)
    for chunk in range(CHUNKS):
        for copy in moves[chunk]:
            copy.wait_recv()

        @pl.loop(chunk * PLANES, (chunk + 1) * PLANES)
        def _(x):
            for comp in range(2):
                for yy in range(4):
                    from_right = rpk3[0, x, comp, yy]
                    from_left = rpk3[1, x, comp, yy]
                    even_rows = jnp.where(odd, from_left, from_right)
                    odd_rows = jnp.where(odd, from_right, from_left)
                    halos = (
                        pltpu.roll(even_rows, 96, axis=1),
                        pltpu.roll(even_rows, 32, axis=1),
                        pltpu.roll(odd_rows, 64, axis=1),
                        odd_rows,
                    )
                    for j in range(4):
                        y = 4 * j + yy
                        out[comp, x, y] = jnp.where(live, jnp.where(middle, out[comp, x, y], halos[j]), 0.0)

    for copy in copies:
        copy.wait_send()


def body(fields, weights, levels, neighbours):
    v = pltpu.VMEM
    dma = pltpu.SemaphoreType.DMA
    hbm = pl.BlockSpec(memory_space=pltpu.HBM)
    return pl.pallas_call(
        kernel,
        out_shape=jax.ShapeDtypeStruct((2, BS, BS, BS, 2 * PER), F32),
        in_specs=[hbm] * 4,
        out_specs=pl.BlockSpec(memory_space=pltpu.VMEM),
        scratch_shapes=[
            v((2, BS, BS, BS, PER), F32),
            v((1, PER), jnp.int32),
            v((1, PER), jnp.int32),
            v((6, PER), jnp.int32),
            v((BS + 2, BS + 2, 32, 128), F32),
            v((BS + 2, BS + 2, 32, 128), F32),
            v((BS + 2, BS + 2, 32, 128), F32),
            v((BS, BS, BS, 128), F32),
            v((2, 3, BS, BS, 128), F32),
            v((6, BS, 32, 128), F32),
            v((6, 2, BS, BS, 128), F32),
            v((8, 128), jnp.int32),
            v((8, 128), F32),
            v((8, 128), F32),
            v((8, 128), F32),
            v((8, 128), F32),
            v((8, 128), F32),
            v((8, 128), F32),
            v((8, 128), F32),
            v((2, 2, 6, 3, 2, BS, 128), F32),
            v((2, 2, 6, 3, 2, BS, 128), F32),
            v((2, BS, 2, 4, BS, 128), F32),
            v((2, BS, 2, 4, BS, 128), F32),
            dma((5,)),
            dma((2, 2, 6)),
            dma((2, 2, 6)),
            dma((2, CHUNKS)),
            dma((2, CHUNKS)),
            dma((PARTNERS,)),
            dma((PARTNERS,)),
            dma((2,)),
            dma((2,)),
        ],
        compiler_params=pltpu.CompilerParams(
            collective_id=0, has_side_effects=True, vmem_limit_bytes=52 << 20
        ),
        cost_estimate=pl.CostEstimate(flops=40_000_000, bytes_accessed=8 << 20, transcendentals=0),
    )(fields, weights.reshape(1, PER), levels.reshape(1, PER), neighbours)


def solution(mesh):
    in_specs = (P(None, None, None, None, "curve"), P("curve"), P("curve"), P(None, "curve"))
    out_specs = P(None, None, None, None, "curve")
    return jax.shard_map(body, mesh=mesh, in_specs=in_specs, out_specs=out_specs, check_vma=False)
```

time: 817 us -> 64.3 us (0.08)
  the two profiles are of different devices: /device:TPU:6 before, /device:TPU:0 now
where the time goes in v1:
time: 64.3 us; the launch traced here: 64.1 us
  Pallas kernels  57.5 us (89%)
  local copies, waits for them, and re-layouts  6.65 us (10%)
    pallas_call x1, Pallas kernels, body(): pl.pallas_call(kernel, out_shape=jax.ShapeDtypeStruct((2, BS, BS, BS, 2 *...  57.5 us
    unnamed x7, local copies, waits for them, and re-layouts  6.65 us

profile of v1, /device:TPU:0, one launch (start us, length us, event | category | flops | bytes accessed | tf_op | source)
XLA Modules:
  0.0 64.1 jit_solution(11387697596352415774)
XLA Ops:
  0.0 0.0 copy-start
  0.0 0.7 %copy-done = s32[6,64]{1,0:T(8,128)S(1)} copy-done((s32[6,64]{1,0:T(8,128)S(1)}, s32[6,64]{1,0:T(8,128)}, u32[]{:S(2)}) %copy-start) | copy-done | bytes 1560
  0.7 0.0 copy-start.1
  0.7 0.7 %copy-done.1 = s32[64]{0:T(128)S(1)} copy-done((s32[64]{0:T(128)S(1)}, s32[64]{0:T(128)}, u32[]{:S(2)}) %copy-start.1) | copy-done | bytes 280
  1.3 0.0 copy-start.2
  1.3 0.7 %copy-done.2 = s32[64]{0:T(128)S(1)} copy-done((s32[64]{0:T(128)S(1)}, s32[64]{0:T(128)}, u32[]{:S(2)}) %copy-start.2) | copy-done | bytes 280
  2.0 57.5 %shard_map.46 = f32[2,16,16,16,128]{4,3,2,1,0:T(8,128)} custom-call(f32[2,16,16,16,64]{4,3,2,1,0:T(8,128)} %fields.1, s32[1,64]{1,0:T(1,128)S(1)} %bitcast.2, s32[1,64]{1,0:T(1,128)S(1)} %bitcast.3, s32[6,64]{1,0:T(8,128)S(1)} %copy-done), custom_call_target="tpu_custom_call" | custom-call | flops 40000000 | bytes 8388608 | tf_op jit(solution)/shard_map/pallas_call | solution.py:352
  59.5 4.7 %copy.6 = f32[2,16,16,16,128]{4,3,2,1,0:T(8,128)} copy(f32[2,16,16,16,128]{4,3,2,1,0:T(8,128)} %shard_map.46) | data formatting | bytes 8388608
Async XLA Ops:
  0.0 0.7 %copy-start = (s32[6,64]{1,0:T(8,128)S(1)}, s32[6,64]{1,0:T(8,128)}, u32[]{:S(2)}) copy-start(s32[6,64]{1,0:T(8,128)} %nbrs.1) | copy-start | bytes 4612
  0.7 0.7 %copy-start.1 = (s32[64]{0:T(128)S(1)}, s32[64]{0:T(128)}, u32[]{:S(2)}) copy-start(s32[64]{0:T(128)} %param.5) | copy-start | bytes 772
  1.3 0.7 %copy-start.2 = (s32[64]{0:T(128)S(1)}, s32[64]{0:T(128)}, u32[]{:S(2)}) copy-start(s32[64]{0:T(128)} %param.6) | copy-start | bytes 772

commit v2 on v1

v2 whole, which is shorter than its diff:
```python
import jax
import jax.numpy as jnp
from jax import lax
from jax.experimental import pallas as pl
from jax.experimental.pallas import tpu as pltpu
from jax.sharding import PartitionSpec as P

MOBILITY_STEP = 0.0006
DIFFUSE_STEP = 0.01
BS = 16
PER = 64
STAGES = ((1, 8), (8, 4), (32, 4))
PARTNERS = sum(size - 1 for _, size in STAGES)
LOADS = 2
PLANES = 2
CHUNKS = BS // PLANES
Z0 = 8
Z1 = Z0 + BS
MESH = pl.DeviceIdType.MESH
F32 = jnp.float32


def kernel(
    fields, weights, levels, nbrs, out,
    raw, wraw, lraw, nraw,
    cp, mp, ep, sf, ftz, turned_own, slab, slab2, ints, kap, wown, wleft, wright, st0, st1, st2,
    spk, rpk, spk3, rpk3,
    in_sem, face_send, face_recv, move_send, move_recv, sum_send, sum_recv, w_send, w_recv,
):
    me = lax.axis_index("curve")
    count = lax.axis_size("curve")
    has_left = me > 0
    has_right = me < count - 1
    left = jnp.maximum(me - 1, 0)
    right = jnp.minimum(me + 1, count - 1)
    sides = ((0, has_left, left, has_right), (1, has_right, right, has_left))
    stage_bufs = (st0, st1, st2)

    def partner(stage, j):
        stride, size = STAGES[stage]
        digit = lax.rem(me // stride, size)
        return me + (lax.rem(digit + j, size) - digit) * stride

    small = [
        pltpu.make_async_copy(weights, wraw, in_sem.at[0]),
        pltpu.make_async_copy(levels, lraw, in_sem.at[1]),
        pltpu.make_async_copy(nbrs, nraw, in_sem.at[2]),
    ]
    loads = []
    for comp in range(2):
        for part in range(LOADS):
            planes = pl.ds(part * (BS // LOADS), BS // LOADS)
            loads.append(pltpu.make_async_copy(fields.at[comp, planes], raw.at[comp, planes], in_sem.at[3 + comp * LOADS + part]))
    for load in small + loads:
        load.start()

    wleft[...] = jnp.zeros((8, 128), F32)
    wright[...] = jnp.zeros((8, 128), F32)

    barrier = pltpu.get_barrier_semaphore()
    for _, there, peer, _ in sides:

        @pl.when(there)
        def _(peer=peer):
            pl.semaphore_signal(barrier, inc=1, device_id=(peer,), device_id_type=MESH)

    for stage, (_, size) in enumerate(STAGES):
        for j in range(1, size):
            pl.semaphore_signal(barrier, inc=1, device_id=(partner(stage, j),), device_id_type=MESH)

    lane = lax.broadcasted_iota(jnp.int32, (BS, 128), 1)
    slot16 = lane // 16
    slot32 = lane // 32

    blank = jnp.zeros((BS, 128), F32)
    for a in range(BS):
        cp[0, 1 + a, Z0:Z1] = blank
        cp[BS + 1, 1 + a, Z0:Z1] = blank
        cp[1 + a, 0, Z0:Z1] = blank
        cp[1 + a, BS + 1, Z0:Z1] = blank
        cp[1 + a, 1 : BS + 1, Z0 - 1] = blank
        cp[1 + a, 1 : BS + 1, Z1] = blank

    ints[...] = jnp.zeros((8, 128), jnp.int32)
    kap[...] = jnp.zeros((8, 128), F32)
    wown[...] = jnp.zeros((8, 128), F32)
    for load in small:
        load.wait()
    ints[0:6, 0:PER] = nraw[...]
    kap[0:1, 0:PER] = 1.0 + 3.0 * lraw[...].astype(F32)
    wown[0:1, 0:PER] = wraw[...].astype(F32)
    kappa = jnp.broadcast_to(kap[0:1], (BS, 128))
    st0[0:1] = jnp.broadcast_to(jnp.sum(wown[0:1], axis=1, keepdims=True), (1, 128))

    for part in range(LOADS):
        loads[part].wait()

        @pl.loop(part * (BS // LOADS), (part + 1) * (BS // LOADS))
        def _(x):
            for y in range(BS):
                cp[x + 1, y + 1, Z0:Z1, 0:PER] = raw[0, x, y]

    for part in range(LOADS):
        loads[LOADS + part].wait()

        @pl.loop(part * (BS // LOADS), (part + 1) * (BS // LOADS))
        def _(x):
            for y in range(BS):
                sf[x, y, :, 0:PER] = raw[1, x, y]

    pl.semaphore_wait(barrier, PARTNERS + has_left.astype(jnp.int32) + has_right.astype(jnp.int32))

    copies = []
    side_copies = []

    def send(src, dst, send_sem, recv_sem, peer):
        copy = pltpu.make_async_remote_copy(
            src_ref=src, dst_ref=dst, send_sem=send_sem, recv_sem=recv_sem,
            device_id=(peer,), device_id_type=MESH,
        )
        copy.start()
        copies.append(copy)
        return copy

    def send_sides(pairs):
        arrivals = []
        for (_, there, peer, source), (src, dst, send_sem, recv_sem) in zip(sides, pairs):
            copy = pltpu.make_async_remote_copy(
                src_ref=src, dst_ref=dst, send_sem=send_sem, recv_sem=recv_sem,
                device_id=(peer,), device_id_type=MESH,
            )
            pl.when(there)(copy.start)
            side_copies.append((there, copy))
            arrivals.append((source, copy))
        return arrivals

    def take_sides(arrivals):
        for source, copy in arrivals:
            pl.when(source)(copy.wait_recv)

    def send_sums(stage):
        buf = stage_bufs[stage]
        base = sum(size - 1 for _, size in STAGES[:stage]) - 1
        return [
            send(buf.at[pl.ds(0, 1)], buf.at[pl.ds(j, 1)], sum_send.at[base + j], sum_recv.at[base + j], partner(stage, j))
            for j in range(1, STAGES[stage][1])
        ]

    def take_sums(stage, arrivals):
        for copy in arrivals:
            copy.wait_recv()
        stride, size = STAGES[stage]
        digit = lax.rem(me // stride, size)
        row = lax.broadcasted_iota(jnp.int32, (8, 128), 0)
        values = stage_bufs[stage][...]
        before = jnp.sum(jnp.where((row >= 1) & (row <= digit), values, 0.0), axis=0, keepdims=True)
        whole = jnp.sum(jnp.where(row < size, values, 0.0), axis=0, keepdims=True)
        return before, whole

    def own(f, layer, a):
        if f >= 4:
            return ftz[f - 4, layer, a]
        depth = 1 if layer == 1 else 0
        at = depth if f % 2 == 0 else BS - 1 - depth
        if f < 2:
            return sf[at, a] if layer == 2 else cp[1 + at, 1 + a, Z0:Z1]
        return sf[a, at] if layer == 2 else cp[1 + a, 1 + at, Z0:Z1]

    def draw_z():
        for a in range(BS):
            ftz[0, 0, a] = cp[1 + a, 1 : BS + 1, Z0]
            ftz[0, 1, a] = cp[1 + a, 1 : BS + 1, Z0 + 1]
            ftz[0, 2, a] = sf[a, :, 0]
            ftz[1, 0, a] = cp[1 + a, 1 : BS + 1, Z1 - 1]
            ftz[1, 1, a] = cp[1 + a, 1 : BS + 1, Z1 - 2]
            ftz[1, 2, a] = sf[a, :, BS - 1]

    def pack_pair(step, pair):
        for f in (2 * pair, 2 * pair + 1):
            for layer in range(3):
                rows = [own(f, layer, a) for a in range(BS)]
                turned = [pltpu.roll(rows[a], 16 * (a // 2), axis=1) if a >= 2 else rows[a] for a in range(BS)]
                to_left, to_right = turned[0:2], turned[0:2]
                for j in range(1, 8):
                    to_left = [jnp.where(slot16 == j, turned[2 * j + aa], to_left[aa]) for aa in range(2)]
                    to_right = [jnp.where(slot16 == (j + 3) % 8, turned[2 * j + aa], to_right[aa]) for aa in range(2)]
                to_left = [pltpu.roll(rows, 64, axis=1) for rows in to_left]
                to_right = [pltpu.roll(rows, 64, axis=1) for rows in to_right]
                for a in range(BS):
                    turned_own[f, layer, a] = turned[a]
                for aa in range(2):
                    spk[step, 0, f, layer, aa] = to_left[aa]
                    spk[step, 1, f, layer, aa] = to_right[aa]
        faces = pl.ds(2 * pair, 2)
        return send_sides([
            (spk.at[step, d, faces], rpk.at[step, d, faces], face_send.at[step, d, pair], face_recv.at[step, d, pair])
            for d in range(2)
        ])

    def ghost_face(step, f):
        g = f ^ 1
        place = jnp.broadcast_to(ints[f : f + 1], (BS, 128))
        inside = place >= 0
        place = place - me * PER
        for layer in range(3):
            from_right = [rpk[step, 0, g, layer, aa] for aa in range(2)]
            from_left = [rpk[step, 1, g, layer, aa] for aa in range(2)]
            table = []
            for a in range(BS):
                rows = jnp.where(slot16 == (a // 2 + 4) % 8, from_right[a % 2], turned_own[g, layer, a])
                table.append(jnp.where(slot16 == (a // 2 + 7) % 8, from_left[a % 2], rows))
            picked = [
                jnp.take_along_axis(table[a], jnp.bitwise_and(place + 16 * (a // 2), 127), axis=1, mode="promise_in_bounds")
                for a in range(BS)
            ]
            ghost = [jnp.where(inside, picked[a], own(f, layer, a)) for a in range(BS)]
            for a in range(BS):
                if layer == 0:
                    slab[f, a, Z0:Z1] = ghost[a]
                    slab[f, a, Z0 - 1 : Z0] = ghost[a][0:1]
                    slab[f, a, Z1 : Z1 + 1] = ghost[a][BS - 1 : BS]
                else:
                    slab2[f, layer - 1, a] = ghost[a]
        done = []
        for a in range(BS):
            g1 = slab[f, a, Z0:Z1]
            g2 = slab2[f, 0, a]
            gs = slab2[f, 1, a]
            around = slab[f, max(a - 1, 0), Z0:Z1] + slab[f, min(a + 1, BS - 1), Z0:Z1]
            around = around + slab[f, a, Z0 - 1 : Z1 - 1] + slab[f, a, Z0 + 1 : Z1 + 1]
            lap = kappa * (g2 + own(f, 0, a) + around - 6.0 * g1)
            square = g1 * g1
            mu = g1 * square - g1 - lap - 0.5 * gs
            excess = gs - 0.5 * square
            done.append((mu, excess, kappa * g1))
        for a in range(BS):
            mu, excess, part = done[a]
            if f < 2:
                edge = 0 if f == 0 else BS + 1
                cell = 1 if f == 0 else BS
                mp[edge, 1 + a, Z0:Z1] = mu
                ep[edge, 1 + a, Z0:Z1] = excess
                mp[cell, 1 + a, Z0:Z1] = mp[cell, 1 + a, Z0:Z1] - part
            elif f < 4:
                edge = 0 if f == 2 else BS + 1
                cell = 1 if f == 2 else BS
                mp[1 + a, edge, Z0:Z1] = mu
                ep[1 + a, edge, Z0:Z1] = excess
                mp[1 + a, cell, Z0:Z1] = mp[1 + a, cell, Z0:Z1] - part
            else:
                edge = Z0 - 1 if f == 4 else Z1
                cell = Z0 if f == 4 else Z1 - 1
                mp[1 + a, 1 : BS + 1, edge] = mu
                ep[1 + a, 1 : BS + 1, edge] = excess
                mp[1 + a, 1 : BS + 1, cell] = mp[1 + a, 1 : BS + 1, cell] - part

    def around_of(ref, x, y):
        total = ref[x, y + 1, Z0:Z1] + ref[x + 2, y + 1, Z0:Z1]
        total = total + ref[x + 1, y, Z0:Z1] + ref[x + 1, y + 2, Z0:Z1]
        return total + ref[x + 1, y + 1, Z0 - 1 : Z1 - 1] + ref[x + 1, y + 1, Z0 + 1 : Z1 + 1]

    def potentials():
        bias = 6.0 * kappa - 1.0

        @pl.loop(0, BS)
        def _(x):
            for y in range(BS):
                c = cp[x + 1, y + 1, Z0:Z1]
                s = sf[x, y]
                square = c * c
                mp[x + 1, y + 1, Z0:Z1] = c * (square + bias) - kappa * around_of(cp, x, y) - 0.5 * s
                ep[x + 1, y + 1, Z0:Z1] = s - 0.5 * square

    c_rate = MOBILITY_STEP * kappa
    s_rate = DIFFUSE_STEP * kappa

    def next_c(x, y):
        return cp[x + 1, y + 1, Z0:Z1] + c_rate * (around_of(mp, x, y) - 6.0 * mp[x + 1, y + 1, Z0:Z1])

    def next_s(x, y):
        return sf[x, y] + s_rate * (around_of(ep, x, y) - 6.0 * ep[x + 1, y + 1, Z0:Z1])

    def exchange_faces(step):
        draw_z()
        arrivals = [pack_pair(step, pair) for pair in range(3)]
        if step == 0:
            row = pl.ds(0, 1)
            sent["w"] = send_sides([
                (wown.at[row], wright.at[row], w_send.at[0], w_recv.at[0]),
                (wown.at[row], wleft.at[row], w_send.at[1], w_recv.at[1]),
            ])
            sent["sums"] = send_sums(0)
        potentials()
        for pair in range(3):
            take_sides(arrivals[pair])
            ghost_face(step, 2 * pair)
            ghost_face(step, 2 * pair + 1)

    sent = {}
    exchange_faces(0)

    before, whole = take_sums(0, sent["sums"])
    st1[0:1] = whole
    sums1 = send_sums(1)

    @pl.loop(0, BS)
    def _(x):
        for y in range(BS):
            cp[x + 1, y + 1, Z0:Z1] = next_c(x, y)
            sf[x, y] = next_s(x, y)

    before1, whole = take_sums(1, sums1)
    st2[0:1] = whole
    sums2 = send_sums(2)
    before = before + before1

    exchange_faces(1)

    turns = (0, 64, 32, 96)
    moves = []
    for chunk in range(CHUNKS):

        @pl.loop(chunk * PLANES, (chunk + 1) * PLANES)
        def _(x):
            for comp, update in ((0, next_c), (1, next_s)):
                for half in range(2):
                    quads = [[update(x, 4 * j + yy) for j in range(4)] for yy in (2 * half, 2 * half + 1)]
                    turned = [[pltpu.roll(q[j], turns[j], axis=1) if turns[j] else q[j] for j in range(4)] for q in quads]
                    shown = [[turned[i][2] if j == 2 else pltpu.roll(quads[i][j], 32, axis=1) for j in range(4)] for i in range(2)]
                    for i in range(2):
                        yy = 2 * half + i
                        u0, u1, u2, u3 = turned[i]
                        spk3[0, x, comp, yy] = jnp.where(slot32 == 0, u0, jnp.where(slot32 == 2, u1, jnp.where(slot32 == 1, u2, u3)))
                        spk3[1, x, comp, yy] = jnp.where(slot32 == 1, u0, jnp.where(slot32 == 3, u1, jnp.where(slot32 == 2, u2, u3)))
                        for j in range(4):
                            out[comp, x, 4 * j + yy] = shown[i][j]

        planes = pl.ds(chunk * PLANES, PLANES)
        moves.append(send_sides([
            (spk3.at[d, planes], rpk3.at[d, planes], move_send.at[d, chunk], move_recv.at[d, chunk]) for d in range(2)
        ]))

    before2, total = take_sums(2, sums2)
    before = before + before2
    take_sides(sent["w"])
    lane1 = lax.broadcasted_iota(jnp.int32, (8, 128), 1)
    ours = jnp.broadcast_to(wown[0:1], (8, 128))
    lefts = jnp.broadcast_to(wleft[0:1], (8, 128))
    rights = jnp.broadcast_to(wright[0:1], (8, 128))
    window = jnp.where(
        (lane1 >= 32) & (lane1 < 96),
        pltpu.roll(ours, 32, axis=1),
        pltpu.roll(jnp.where(lane1 < 32, rights, lefts), 96, axis=1),
    )
    earlier = (lax.broadcasted_iota(jnp.int32, (128, 128), 0) < lax.broadcasted_iota(jnp.int32, (128, 128), 1)).astype(F32)
    upto = jnp.dot(window, earlier, preferred_element_type=F32)
    lead = jnp.sum(jnp.where(lane1 < 32, window, 0.0), axis=1, keepdims=True)
    prior = (jnp.broadcast_to(before, (8, 128)) - lead + upto).astype(jnp.int32) * count
    whole_sum = jnp.broadcast_to(total, (8, 128)).astype(jnp.int32)
    live8 = (prior >= me * whole_sum) & (prior < (me + 1) * whole_sum)
    block = me * PER - 32 + lane1
    live8 = live8 & (block >= 0) & (block < count * PER)
    live = jnp.broadcast_to(live8.astype(F32)[0:1], (BS, 128)) > 0.5

    odd = jnp.bitwise_and(slot32, 1) == 1
    middle = (lane >= 32) & (lane < 96)
    for chunk in range(CHUNKS):
        take_sides(moves[chunk])

        @pl.loop(chunk * PLANES, (chunk + 1) * PLANES)
        def _(x):
            for comp in range(2):
                from_right = [rpk3[0, x, comp, yy] for yy in range(4)]
                from_left = [rpk3[1, x, comp, yy] for yy in range(4)]
                even_rows = [jnp.where(odd, from_left[yy], from_right[yy]) for yy in range(4)]
                odd_rows = [jnp.where(odd, from_right[yy], from_left[yy]) for yy in range(4)]
                halos = [
                    [pltpu.roll(rows, 96, axis=1) for rows in even_rows],
                    [pltpu.roll(rows, 32, axis=1) for rows in even_rows],
                    [pltpu.roll(rows, 64, axis=1) for rows in odd_rows],
                    odd_rows,
                ]
                merged = [jnp.where(live, jnp.where(middle, out[comp, x, y], halos[y // 4][y % 4]), 0.0) for y in range(BS)]
                for y in range(BS):
                    out[comp, x, y] = merged[y]

    for copy in copies:
        copy.wait_send()
    for there, copy in side_copies:
        pl.when(there)(copy.wait_send)


def store_kernel(window, out, sems):
    parts = 4
    copies = [
        pltpu.make_async_copy(
            window.at[k // 2, pl.ds((k % 2) * 8, 8)], out.at[k // 2, pl.ds((k % 2) * 8, 8)], sems.at[k]
        )
        for k in range(parts)
    ]
    for copy in copies:
        copy.start()
    for copy in copies:
        copy.wait()


def body(fields, weights, levels, neighbours):
    v = pltpu.VMEM
    dma = pltpu.SemaphoreType.DMA
    hbm = pl.BlockSpec(memory_space=pltpu.HBM)
    fields, weights, levels, neighbours = (
        pltpu.with_memory_space_constraint(x, pltpu.HBM)
        for x in (fields, weights.reshape(1, PER), levels.reshape(1, PER), neighbours)
    )
    window = pl.pallas_call(
        kernel,
        out_shape=pltpu.VMEM((2, BS, BS, BS, 2 * PER), F32),
        in_specs=[hbm] * 4,
        out_specs=pl.BlockSpec(memory_space=pltpu.VMEM),
        scratch_shapes=[
            v((2, BS, BS, BS, PER), F32),
            v((1, PER), jnp.int32),
            v((1, PER), jnp.int32),
            v((6, PER), jnp.int32),
            v((BS + 2, BS + 2, 32, 128), F32),
            v((BS + 2, BS + 2, 32, 128), F32),
            v((BS + 2, BS + 2, 32, 128), F32),
            v((BS, BS, BS, 128), F32),
            v((2, 3, BS, BS, 128), F32),
            v((6, 3, BS, BS, 128), F32),
            v((6, BS, 32, 128), F32),
            v((6, 2, BS, BS, 128), F32),
            v((8, 128), jnp.int32),
            v((8, 128), F32),
            v((8, 128), F32),
            v((8, 128), F32),
            v((8, 128), F32),
            v((8, 128), F32),
            v((8, 128), F32),
            v((8, 128), F32),
            v((2, 2, 6, 3, 2, BS, 128), F32),
            v((2, 2, 6, 3, 2, BS, 128), F32),
            v((2, BS, 2, 4, BS, 128), F32),
            v((2, BS, 2, 4, BS, 128), F32),
            dma((3 + 2 * LOADS,)),
            dma((2, 2, 3)),
            dma((2, 2, 3)),
            dma((2, CHUNKS)),
            dma((2, CHUNKS)),
            dma((PARTNERS,)),
            dma((PARTNERS,)),
            dma((2,)),
            dma((2,)),
        ],
        compiler_params=pltpu.CompilerParams(
            collective_id=0, has_side_effects=True, vmem_limit_bytes=44 << 20
        ),
        cost_estimate=pl.CostEstimate(flops=40_000_000, bytes_accessed=8 << 20, transcendentals=0),
    )(fields, weights, levels, neighbours)
    return pl.pallas_call(
        store_kernel,
        out_shape=jax.ShapeDtypeStruct((2, BS, BS, BS, 2 * PER), F32),
        in_specs=[pl.BlockSpec(memory_space=pltpu.VMEM)],
        out_specs=pl.BlockSpec(memory_space=pltpu.HBM),
        scratch_shapes=[dma((4,))],
        compiler_params=pltpu.CompilerParams(vmem_limit_bytes=8 << 20),
    )(pltpu.with_memory_space_constraint(window, pltpu.VMEM))


def solution(mesh):
    in_specs = (P(None, None, None, None, "curve"), P("curve"), P("curve"), P(None, "curve"))
    out_specs = P(None, None, None, None, "curve")
    return jax.shard_map(body, mesh=mesh, in_specs=in_specs, out_specs=out_specs, check_vma=False)
```

time: 64.3 us -> 45.4 us (0.71)
  the two profiles are of different devices: /device:TPU:0 before, /device:TPU:6 now
where the time goes in v2:
time: 45.4 us; the launch traced here: 45.2 us
  Pallas kernels  45.2 us (100%)
    pallas_call x1, Pallas kernels, body(): pl.pallas_call(kernel, out_shape=pltpu.VMEM((2, BS, BS, BS, 2 * PER), F32...  43.2 us
    pallas_call x1, Pallas kernels, body(): pl.pallas_call(store_kernel, out_shape=jax.ShapeDtypeStruct((2, BS, BS, B...  2.04 us

profile of v2, /device:TPU:6, one launch (start us, length us, event | category | flops | bytes accessed | tf_op | source)
XLA Modules:
  0.0 45.2 jit_solution(2189760276913958510)
XLA Ops:
  0.0 43.2 %shard_map.46.window = f32[2,16,16,16,128]{4,3,2,1,0:T(8,128)S(1)} custom-call(f32[2,16,16,16,64]{4,3,2,1,0:T(8,128)} %fields.1, s32[1,64]{1,0:T(1,128)} %bitcast.2, s32[1,64]{1,0:T(1,128)} %bitcast.3, s32[6,64]{1,0:T(8,128)} %nbrs.1), custom_call_target="tpu_custom_call" | custom-call | flops 40000000 | bytes 8388608 | tf_op jit(solution)/shard_map/pallas_call | solution.py:415
  43.2 2.0 %shard_map.47 = f32[2,16,16,16,128]{4,3,2,1,0:T(8,128)} custom-call(f32[2,16,16,16,128]{4,3,2,1,0:T(8,128)S(1)} %shard_map.46.window), custom_call_target="tpu_custom_call" | custom-call | tf_op jit(solution)/shard_map/pallas_call | solution.py:460

commit v3 on v2

--- a/solution.py
+++ b/solution.py
@@ -12,8 +12,11 @@
 STAGES = ((1, 8), (8, 4), (32, 4))
 PARTNERS = sum(size - 1 for _, size in STAGES)
 LOADS = 2
-PLANES = 2
-CHUNKS = BS // PLANES
+RIM = (0, 1, BS - 2, BS - 1)
+INNER = (2, BS - 2)
+INNER_CHUNKS = 4
+INNER_PLANES = 12 // INNER_CHUNKS
+CHUNKS = INNER_CHUNKS + 3
 Z0 = 8
 Z1 = Z0 + BS
 MESH = pl.DeviceIdType.MESH
@@ -23,17 +26,18 @@
 def kernel(
     fields, weights, levels, nbrs, out,
     raw, wraw, lraw, nraw,
-    cp, mp, ep, sf, ftz, turned_own, slab, slab2, ints, kap, wown, wleft, wright, st0, st1, st2,
-    spk, rpk, spk3, rpk3,
+    cp, mp, ep, sf, ftz, turned_own, slab, slab2, ints, kap, wown, wnear, st0, st1, st2,
+    spk, rpk, spk_in, rpk_in, spk_mid, rpk_mid, spk_out, rpk_out,
     in_sem, face_send, face_recv, move_send, move_recv, sum_send, sum_recv, w_send, w_recv,
 ):
     me = lax.axis_index("curve")
     count = lax.axis_size("curve")
-    has_left = me > 0
-    has_right = me < count - 1
-    left = jnp.maximum(me - 1, 0)
-    right = jnp.minimum(me + 1, count - 1)
-    sides = ((0, has_left, left, has_right), (1, has_right, right, has_left))
+    first = me == 0
+    last = me == count - 1
+    left = jnp.where(first, 1, me - 1)
+    right = jnp.where(last, count - 2, me + 1)
+    spare = (me == 1) | (me == count - 2)
+    sides = ((left, jnp.where(first, 2, 0)), (right, jnp.where(last, 2, 1)))
     stage_bufs = (st0, st1, st2)
 
     def partner(stage, j):
@@ -54,16 +58,9 @@
     for load in small + loads:
         load.start()
 
-    wleft[...] = jnp.zeros((8, 128), F32)
-    wright[...] = jnp.zeros((8, 128), F32)
-
     barrier = pltpu.get_barrier_semaphore()
-    for _, there, peer, _ in sides:
-
-        @pl.when(there)
-        def _(peer=peer):
-            pl.semaphore_signal(barrier, inc=1, device_id=(peer,), device_id_type=MESH)
-
+    for peer in (left, right):
+        pl.semaphore_signal(barrier, inc=1, device_id=(peer,), device_id_type=MESH)
     for stage, (_, size) in enumerate(STAGES):
         for j in range(1, size):
             pl.semaphore_signal(barrier, inc=1, device_id=(partner(stage, j),), device_id_type=MESH)
@@ -108,10 +105,9 @@
             for y in range(BS):
                 sf[x, y, :, 0:PER] = raw[1, x, y]
 
-    pl.semaphore_wait(barrier, PARTNERS + has_left.astype(jnp.int32) + has_right.astype(jnp.int32))
+    pl.semaphore_wait(barrier, PARTNERS + 2 + spare.astype(jnp.int32) - (first | last).astype(jnp.int32))
 
     copies = []
-    side_copies = []
 
     def send(src, dst, send_sem, recv_sem, peer):
         copy = pltpu.make_async_remote_copy(
@@ -122,21 +118,47 @@
         copies.append(copy)
         return copy
 
-    def send_sides(pairs):
-        arrivals = []
-        for (_, there, peer, source), (src, dst, send_sem, recv_sem) in zip(sides, pairs):
-            copy = pltpu.make_async_remote_copy(
-                src_ref=src, dst_ref=dst, send_sem=send_sem, recv_sem=recv_sem,
-                device_id=(peer,), device_id_type=MESH,
-            )
-            pl.when(there)(copy.start)
-            side_copies.append((there, copy))
-            arrivals.append((source, copy))
-        return arrivals
-
-    def take_sides(arrivals):
-        for source, copy in arrivals:
-            pl.when(source)(copy.wait_recv)
+    def near(kind, d, slot):
+        name, *at = kind
+        if name == "face":
+            step, pair = at
+            faces = pl.ds(2 * pair, 2)
+            return spk.at[step, d, faces], rpk.at[step, slot, faces], face_send.at[step, d, pair], face_recv.at[step, slot, pair]
+        if name == "weights":
+            row = pl.ds(0, 1)
+            return wown.at[row], wnear.at[slot, row], w_send.at[d], w_recv.at[slot]
+        (chunk,) = at
+        sems = move_send.at[d, chunk], move_recv.at[slot, chunk]
+        if chunk < INNER_CHUNKS:
+            planes = pl.ds(chunk * INNER_PLANES, INNER_PLANES)
+            return spk_in.at[d, planes], rpk_in.at[slot, planes], *sems
+        if chunk == INNER_CHUNKS:
+            return spk_mid.at[d], rpk_mid.at[slot], *sems
+        planes = pl.ds(2 * (chunk - INNER_CHUNKS - 1), 2)
+        return spk_out.at[d, planes], rpk_out.at[slot, planes], *sems
+
+    kinds = [("face", step, pair) for step in range(2) for pair in range(3)]
+    kinds += [("weights",)] + [("move", chunk) for chunk in range(CHUNKS)]
+
+    for end, slot in ((first, 1), (last, 0)):
+
+        @pl.when(end)
+        def _(slot=slot):
+            for kind in kinds:
+                _, place, _, sem = near(kind, 0, slot)
+                pltpu.make_async_copy(near(kind, 0, 2)[1], place, sem).start()
+
+    def send_sides(kind):
+        for d, (peer, slot) in enumerate(sides):
+            send(*near(kind, d, slot), peer)
+
+    def take(kind, slot):
+        src, place, send_sem, recv_sem = near(kind, 0, slot)
+        pltpu.make_async_copy(place, place, recv_sem).wait()
+
+    def take_sides(kind):
+        take(kind, 0)
+        take(kind, 1)
 
     def send_sums(stage):
         buf = stage_bufs[stage]
@@ -191,11 +213,7 @@
                 for aa in range(2):
                     spk[step, 0, f, layer, aa] = to_left[aa]
                     spk[step, 1, f, layer, aa] = to_right[aa]
-        faces = pl.ds(2 * pair, 2)
-        return send_sides([
-            (spk.at[step, d, faces], rpk.at[step, d, faces], face_send.at[step, d, pair], face_recv.at[step, d, pair])
-            for d in range(2)
-        ])
+        send_sides(("face", step, pair))
 
     def ghost_face(step, f):
         g = f ^ 1
@@ -280,114 +298,165 @@
     def next_s(x, y):
         return sf[x, y] + s_rate * (around_of(ep, x, y) - 6.0 * ep[x + 1, y + 1, Z0:Z1])
 
-    def exchange_faces(step):
+    def send_faces(step):
         draw_z()
-        arrivals = [pack_pair(step, pair) for pair in range(3)]
-        if step == 0:
-            row = pl.ds(0, 1)
-            sent["w"] = send_sides([
-                (wown.at[row], wright.at[row], w_send.at[0], w_recv.at[0]),
-                (wown.at[row], wleft.at[row], w_send.at[1], w_recv.at[1]),
-            ])
-            sent["sums"] = send_sums(0)
-        potentials()
-        for pair in range(3):
-            take_sides(arrivals[pair])
-            ghost_face(step, 2 * pair)
-            ghost_face(step, 2 * pair + 1)
-
-    sent = {}
-    exchange_faces(0)
-
-    before, whole = take_sums(0, sent["sums"])
+        for pair in (2, 0, 1):
+            pack_pair(step, pair)
+
+    def take_faces(step, pair):
+        take_sides(("face", step, pair))
+        ghost_face(step, 2 * pair)
+        ghost_face(step, 2 * pair + 1)
+
+    def renew(x, ys):
+        for y in ys:
+            cp[x + 1, y + 1, Z0:Z1] = next_c(x, y)
+            sf[x, y] = next_s(x, y)
+
+    send_faces(0)
+    send_sides(("weights",))
+    sums0 = send_sums(0)
+    potentials()
+    take_faces(0, 2)
+
+    @pl.loop(*INNER)
+    def _(x):
+        renew(x, range(*INNER))
+
+    before, whole = take_sums(0, sums0)
     st1[0:1] = whole
     sums1 = send_sums(1)
-
-    @pl.loop(0, BS)
+    take_faces(0, 0)
+    take_faces(0, 1)
+
+    @pl.loop(*INNER)
     def _(x):
-        for y in range(BS):
-            cp[x + 1, y + 1, Z0:Z1] = next_c(x, y)
-            sf[x, y] = next_s(x, y)
+        renew(x, RIM)
+
+    for x in RIM:
+        renew(x, range(BS))
 
     before1, whole = take_sums(1, sums1)
     st2[0:1] = whole
     sums2 = send_sums(2)
     before = before + before1
 
-    exchange_faces(1)
+    send_faces(1)
+    potentials()
+    take_faces(1, 2)
 
     turns = (0, 64, 32, 96)
-    moves = []
-    for chunk in range(CHUNKS):
-
-        @pl.loop(chunk * PLANES, (chunk + 1) * PLANES)
-        def _(x):
-            for comp, update in ((0, next_c), (1, next_s)):
-                for half in range(2):
-                    quads = [[update(x, 4 * j + yy) for j in range(4)] for yy in (2 * half, 2 * half + 1)]
-                    turned = [[pltpu.roll(q[j], turns[j], axis=1) if turns[j] else q[j] for j in range(4)] for q in quads]
-                    shown = [[turned[i][2] if j == 2 else pltpu.roll(quads[i][j], 32, axis=1) for j in range(4)] for i in range(2)]
-                    for i in range(2):
-                        yy = 2 * half + i
-                        u0, u1, u2, u3 = turned[i]
-                        spk3[0, x, comp, yy] = jnp.where(slot32 == 0, u0, jnp.where(slot32 == 2, u1, jnp.where(slot32 == 1, u2, u3)))
-                        spk3[1, x, comp, yy] = jnp.where(slot32 == 1, u0, jnp.where(slot32 == 3, u1, jnp.where(slot32 == 2, u2, u3)))
-                        for j in range(4):
-                            out[comp, x, 4 * j + yy] = shown[i][j]
-
-        planes = pl.ds(chunk * PLANES, PLANES)
-        moves.append(send_sides([
-            (spk3.at[d, planes], rpk3.at[d, planes], move_send.at[d, chunk], move_recv.at[d, chunk]) for d in range(2)
-        ]))
+
+    def quad(yy):
+        return RIM if yy == 3 else tuple(2 + yy + 3 * j for j in range(4))
+
+    def evolve(x, groups, packed, plane):
+        for comp, update in ((0, next_c), (1, next_s)):
+            for some in (groups[:2], groups[2:]):
+                quads = [[update(x, y) for y in quad(yy)] for yy in some]
+                turned = [[pltpu.roll(q[j], turns[j], axis=1) if turns[j] else q[j] for j in range(4)] for q in quads]
+                shown = [[turned[i][2] if j == 2 else pltpu.roll(q[j], 32, axis=1) for j in range(4)] for i, q in enumerate(quads)]
+                for i, yy in enumerate(some):
+                    u0, u1, u2, u3 = turned[i]
+                    row = groups.index(yy)
+                    packed[0, plane, comp, row] = jnp.where(slot32 == 0, u0, jnp.where(slot32 == 2, u1, jnp.where(slot32 == 1, u2, u3)))
+                    packed[1, plane, comp, row] = jnp.where(slot32 == 1, u0, jnp.where(slot32 == 3, u1, jnp.where(slot32 == 2, u2, u3)))
+                    for j, y in enumerate(quad(yy)):
+                        out[comp, x, y] = shown[i][j]
+
+    for chunk in range(INNER_CHUNKS):
+
+        @pl.loop(chunk * INNER_PLANES, (chunk + 1) * INNER_PLANES)
+        def _(plane):
+            evolve(plane + 2, (0, 1, 2), spk_in, plane)
+
+        send_sides(("move", chunk))
+
+    take_faces(1, 0)
+    take_faces(1, 1)
+
+    @pl.loop(0, 12)
+    def _(plane):
+        evolve(plane + 2, (3,), spk_mid, plane)
+
+    send_sides(("move", INNER_CHUNKS))
+    for part in range(2):
+        for k in (2 * part, 2 * part + 1):
+            evolve(RIM[k], (0, 1, 2, 3), spk_out, k)
+        send_sides(("move", INNER_CHUNKS + 1 + part))
 
     before2, total = take_sums(2, sums2)
     before = before + before2
-    take_sides(sent["w"])
+    take_sides(("weights",))
     lane1 = lax.broadcasted_iota(jnp.int32, (8, 128), 1)
     ours = jnp.broadcast_to(wown[0:1], (8, 128))
-    lefts = jnp.broadcast_to(wleft[0:1], (8, 128))
-    rights = jnp.broadcast_to(wright[0:1], (8, 128))
+    lefts = jnp.broadcast_to(wnear[1, 0:1], (8, 128))
+    rights = jnp.broadcast_to(wnear[0, 0:1], (8, 128))
+    block = me * PER - 32 + lane1
+    exists = (block >= 0) & (block < count * PER)
     window = jnp.where(
         (lane1 >= 32) & (lane1 < 96),
         pltpu.roll(ours, 32, axis=1),
         pltpu.roll(jnp.where(lane1 < 32, rights, lefts), 96, axis=1),
     )
+    window = jnp.where(exists, window, 0.0)
     earlier = (lax.broadcasted_iota(jnp.int32, (128, 128), 0) < lax.broadcasted_iota(jnp.int32, (128, 128), 1)).astype(F32)
     upto = jnp.dot(window, earlier, preferred_element_type=F32)
     lead = jnp.sum(jnp.where(lane1 < 32, window, 0.0), axis=1, keepdims=True)
     prior = (jnp.broadcast_to(before, (8, 128)) - lead + upto).astype(jnp.int32) * count
     whole_sum = jnp.broadcast_to(total, (8, 128)).astype(jnp.int32)
     live8 = (prior >= me * whole_sum) & (prior < (me + 1) * whole_sum)
-    block = me * PER - 32 + lane1
-    live8 = live8 & (block >= 0) & (block < count * PER)
+    live8 = live8 & exists
     live = jnp.broadcast_to(live8.astype(F32)[0:1], (BS, 128)) > 0.5
 
     odd = jnp.bitwise_and(slot32, 1) == 1
     middle = (lane >= 32) & (lane < 96)
-    for chunk in range(CHUNKS):
-        take_sides(moves[chunk])
-
-        @pl.loop(chunk * PLANES, (chunk + 1) * PLANES)
-        def _(x):
-            for comp in range(2):
-                from_right = [rpk3[0, x, comp, yy] for yy in range(4)]
-                from_left = [rpk3[1, x, comp, yy] for yy in range(4)]
-                even_rows = [jnp.where(odd, from_left[yy], from_right[yy]) for yy in range(4)]
-                odd_rows = [jnp.where(odd, from_right[yy], from_left[yy]) for yy in range(4)]
-                halos = [
-                    [pltpu.roll(rows, 96, axis=1) for rows in even_rows],
-                    [pltpu.roll(rows, 32, axis=1) for rows in even_rows],
-                    [pltpu.roll(rows, 64, axis=1) for rows in odd_rows],
-                    odd_rows,
-                ]
-                merged = [jnp.where(live, jnp.where(middle, out[comp, x, y], halos[y // 4][y % 4]), 0.0) for y in range(BS)]
-                for y in range(BS):
-                    out[comp, x, y] = merged[y]
+
+    def settle(x, groups, packed, plane):
+        for comp in range(2):
+            from_right = [packed[0, plane, comp, row] for row in range(len(groups))]
+            from_left = [packed[1, plane, comp, row] for row in range(len(groups))]
+            even_rows = [jnp.where(odd, a, b) for a, b in zip(from_left, from_right)]
+            odd_rows = [jnp.where(odd, b, a) for a, b in zip(from_left, from_right)]
+            halos = [
+                [pltpu.roll(rows, 96, axis=1) for rows in even_rows],
+                [pltpu.roll(rows, 32, axis=1) for rows in even_rows],
+                [pltpu.roll(rows, 64, axis=1) for rows in odd_rows],
+                odd_rows,
+            ]
+            merged = [
+                (y, jnp.where(live, jnp.where(middle, out[comp, x, y], halos[j][row]), 0.0))
+                for row, yy in enumerate(groups)
+                for j, y in enumerate(quad(yy))
+            ]
+            for y, value in merged:
+                out[comp, x, y] = value
+
+    for chunk in range(INNER_CHUNKS):
+        take_sides(("move", chunk))
+
+        @pl.loop(chunk * INNER_PLANES, (chunk + 1) * INNER_PLANES)
+        def _(plane):
+            settle(plane + 2, (0, 1, 2), rpk_in, plane)
+
+    take_sides(("move", INNER_CHUNKS))
+
+    @pl.loop(0, 12)
+    def _(plane):
+        settle(plane + 2, (3,), rpk_mid, plane)
+
+    for part in range(2):
+        take_sides(("move", INNER_CHUNKS + 1 + part))
+        for k in (2 * part, 2 * part + 1):
+            settle(RIM[k], (0, 1, 2, 3), rpk_out, k)
 
     for copy in copies:
         copy.wait_send()
-    for there, copy in side_copies:
-        pl.when(there)(copy.wait_send)
+
+    @pl.when(spare)
+    def _():
+        for kind in kinds:
+            take(kind, 2)
 
 
 def store_kernel(window, out, sems):
@@ -433,24 +502,27 @@
             v((8, 128), jnp.int32),
             v((8, 128), F32),
             v((8, 128), F32),
-            v((8, 128), F32),
-            v((8, 128), F32),
+            v((3, 8, 128), F32),
             v((8, 128), F32),
             v((8, 128), F32),
             v((8, 128), F32),
             v((2, 2, 6, 3, 2, BS, 128), F32),
-            v((2, 2, 6, 3, 2, BS, 128), F32),
-            v((2, BS, 2, 4, BS, 128), F32),
-            v((2, BS, 2, 4, BS, 128), F32),
+            v((2, 3, 6, 3, 2, BS, 128), F32),
+            v((2, 12, 2, 3, BS, 128), F32),
+            v((3, 12, 2, 3, BS, 128), F32),
+            v((2, 12, 2, 1, BS, 128), F32),
+            v((3, 12, 2, 1, BS, 128), F32),
+            v((2, 4, 2, 4, BS, 128), F32),
+            v((3, 4, 2, 4, BS, 128), F32),
             dma((3 + 2 * LOADS,)),
             dma((2, 2, 3)),
-            dma((2, 2, 3)),
+            dma((2, 3, 3)),
             dma((2, CHUNKS)),
-            dma((2, CHUNKS)),
+            dma((3, CHUNKS)),
             dma((PARTNERS,)),
             dma((PARTNERS,)),
             dma((2,)),
-            dma((2,)),
+            dma((3,)),
         ],
         compiler_params=pltpu.CompilerParams(
             collective_id=0, has_side_effects=True, vmem_limit_bytes=44 << 20

time: 45.4 us -> 42.9 us (0.945)
  Pallas kernels: 45.2 us -> 42.8 us
    pallas_call x1, Pallas kernels: 43.2 us -> 40.8 us  [body(): pl.pallas_call(kernel, out_shape=pltpu.VMEM((2, BS, BS, BS, 2 * PER), F32...]
where the time goes in v3:
time: 42.9 us; the launch traced here: 42.8 us
  Pallas kernels  42.8 us (100%)
    pallas_call x1, Pallas kernels, body(): pl.pallas_call(kernel, out_shape=pltpu.VMEM((2, BS, BS, BS, 2 * PER), F32...  40.8 us
    pallas_call x1, Pallas kernels, body(): pl.pallas_call(store_kernel, out_shape=jax.ShapeDtypeStruct((2, BS, BS, B...  2.04 us

profile of v3, /device:TPU:6, one launch (start us, length us, event | category | flops | bytes accessed | tf_op | source)
XLA Modules:
  0.0 42.8 jit_solution(11501160269008224857)
XLA Ops:
  0.0 40.8 %shard_map.46.window = f32[2,16,16,16,128]{4,3,2,1,0:T(8,128)S(1)} custom-call(f32[2,16,16,16,64]{4,3,2,1,0:T(8,128)} %fields.1, s32[1,64]{1,0:T(1,128)} %bitcast.2, s32[1,64]{1,0:T(1,128)} %bitcast.3, s32[6,64]{1,0:T(8,128)} %nbrs.1), custom_call_target="tpu_custom_call" | custom-call | flops 40000000 | bytes 8388608 | tf_op jit(solution)/shard_map/pallas_call | solution.py:484
  40.8 2.0 %shard_map.47 = f32[2,16,16,16,128]{4,3,2,1,0:T(8,128)} custom-call(f32[2,16,16,16,128]{4,3,2,1,0:T(8,128)S(1)} %shard_map.46.window), custom_call_target="tpu_custom_call" | custom-call | tf_op jit(solution)/shard_map/pallas_call | solution.py:532

commit v4 on v3

--- a/solution.py
+++ b/solution.py
@@ -14,8 +14,8 @@
 LOADS = 2
 RIM = (0, 1, BS - 2, BS - 1)
 INNER = (2, BS - 2)
-INNER_CHUNKS = 4
-INNER_PLANES = 12 // INNER_CHUNKS
+INNER_CUTS = (0, 1, 4, 8, 12)
+INNER_CHUNKS = len(INNER_CUTS) - 1
 CHUNKS = INNER_CHUNKS + 3
 Z0 = 8
 Z1 = Z0 + BS
@@ -105,7 +105,6 @@
             for y in range(BS):
                 sf[x, y, :, 0:PER] = raw[1, x, y]
 
-    pl.semaphore_wait(barrier, PARTNERS + 2 + spare.astype(jnp.int32) - (first | last).astype(jnp.int32))
 
     copies = []
 
@@ -130,7 +129,7 @@
         (chunk,) = at
         sems = move_send.at[d, chunk], move_recv.at[slot, chunk]
         if chunk < INNER_CHUNKS:
-            planes = pl.ds(chunk * INNER_PLANES, INNER_PLANES)
+            planes = pl.ds(INNER_CUTS[chunk], INNER_CUTS[chunk + 1] - INNER_CUTS[chunk])
             return spk_in.at[d, planes], rpk_in.at[slot, planes], *sems
         if chunk == INNER_CHUNKS:
             return spk_mid.at[d], rpk_mid.at[slot], *sems
@@ -139,14 +138,6 @@
 
     kinds = [("face", step, pair) for step in range(2) for pair in range(3)]
     kinds += [("weights",)] + [("move", chunk) for chunk in range(CHUNKS)]
-
-    for end, slot in ((first, 1), (last, 0)):
-
-        @pl.when(end)
-        def _(slot=slot):
-            for kind in kinds:
-                _, place, _, sem = near(kind, 0, slot)
-                pltpu.make_async_copy(near(kind, 0, 2)[1], place, sem).start()
 
     def send_sides(kind):
         for d, (peer, slot) in enumerate(sides):
@@ -213,7 +204,6 @@
                 for aa in range(2):
                     spk[step, 0, f, layer, aa] = to_left[aa]
                     spk[step, 1, f, layer, aa] = to_right[aa]
-        send_sides(("face", step, pair))
 
     def ghost_face(step, f):
         g = f ^ 1
@@ -299,9 +289,10 @@
         return sf[x, y] + s_rate * (around_of(ep, x, y) - 6.0 * ep[x + 1, y + 1, Z0:Z1])
 
     def send_faces(step):
-        draw_z()
-        for pair in (2, 0, 1):
+        send_sides(("face", step, 2))
+        for pair in (0, 1):
             pack_pair(step, pair)
+            send_sides(("face", step, pair))
 
     def take_faces(step, pair):
         take_sides(("face", step, pair))
@@ -313,36 +304,45 @@
             cp[x + 1, y + 1, Z0:Z1] = next_c(x, y)
             sf[x, y] = next_s(x, y)
 
+    draw_z()
+    pack_pair(0, 2)
+    pl.semaphore_wait(barrier, PARTNERS + 2 + spare.astype(jnp.int32) - (first | last).astype(jnp.int32))
     send_faces(0)
     send_sides(("weights",))
+    potentials()
     sums0 = send_sums(0)
-    potentials()
+
+    for end, slot in ((first, 1), (last, 0)):
+
+        @pl.when(end)
+        def _(slot=slot):
+            for kind in kinds:
+                _, place, _, sem = near(kind, 0, slot)
+                pltpu.make_async_copy(near(kind, 0, 2)[1], place, sem).start()
+
     take_faces(0, 2)
 
     @pl.loop(*INNER)
     def _(x):
         renew(x, range(*INNER))
 
+    take_faces(0, 0)
+    take_faces(0, 1)
+
+    @pl.loop(*INNER)
+    def _(x):
+        renew(x, RIM)
+
+    for x in RIM:
+        renew(x, range(BS))
+
+    draw_z()
+    pack_pair(1, 2)
+    send_faces(1)
+    potentials()
     before, whole = take_sums(0, sums0)
     st1[0:1] = whole
     sums1 = send_sums(1)
-    take_faces(0, 0)
-    take_faces(0, 1)
-
-    @pl.loop(*INNER)
-    def _(x):
-        renew(x, RIM)
-
-    for x in RIM:
-        renew(x, range(BS))
-
-    before1, whole = take_sums(1, sums1)
-    st2[0:1] = whole
-    sums2 = send_sums(2)
-    before = before + before1
-
-    send_faces(1)
-    potentials()
     take_faces(1, 2)
 
     turns = (0, 64, 32, 96)
@@ -366,12 +366,16 @@
 
     for chunk in range(INNER_CHUNKS):
 
-        @pl.loop(chunk * INNER_PLANES, (chunk + 1) * INNER_PLANES)
+        @pl.loop(INNER_CUTS[chunk], INNER_CUTS[chunk + 1])
         def _(plane):
             evolve(plane + 2, (0, 1, 2), spk_in, plane)
 
         send_sides(("move", chunk))
 
+    before1, whole = take_sums(1, sums1)
+    st2[0:1] = whole
+    sums2 = send_sums(2)
+    before = before + before1
     take_faces(1, 0)
     take_faces(1, 1)
 
@@ -435,7 +439,7 @@
     for chunk in range(INNER_CHUNKS):
         take_sides(("move", chunk))
 
-        @pl.loop(chunk * INNER_PLANES, (chunk + 1) * INNER_PLANES)
+        @pl.loop(INNER_CUTS[chunk], INNER_CUTS[chunk + 1])
         def _(plane):
             settle(plane + 2, (0, 1, 2), rpk_in, plane)
 

time: 42.9 us -> 41.7 us (0.972)
  Pallas kernels: 42.8 us -> 41.6 us
    pallas_call x1, Pallas kernels: 40.8 us -> 39.6 us  [body(): pl.pallas_call(kernel, out_shape=pltpu.VMEM((2, BS, BS, BS, 2 * PER), F32...]
where the time goes in v4:
time: 41.7 us; the launch traced here: 41.6 us
  Pallas kernels  41.6 us (100%)
    pallas_call x1, Pallas kernels, body(): pl.pallas_call(kernel, out_shape=pltpu.VMEM((2, BS, BS, BS, 2 * PER), F32...  39.6 us
    pallas_call x1, Pallas kernels, body(): pl.pallas_call(store_kernel, out_shape=jax.ShapeDtypeStruct((2, BS, BS, B...  2.04 us

profile of v4, /device:TPU:6, one launch (start us, length us, event | category | flops | bytes accessed | tf_op | source)
XLA Modules:
  0.0 41.6 jit_solution(2260288964988654506)
XLA Ops:
  0.0 39.6 %shard_map.46.window = f32[2,16,16,16,128]{4,3,2,1,0:T(8,128)S(1)} custom-call(f32[2,16,16,16,64]{4,3,2,1,0:T(8,128)} %fields.1, s32[1,64]{1,0:T(1,128)} %bitcast.2, s32[1,64]{1,0:T(1,128)} %bitcast.3, s32[6,64]{1,0:T(8,128)} %nbrs.1), custom_call_target="tpu_custom_call" | custom-call | flops 40000000 | bytes 8388608 | tf_op jit(solution)/shard_map/pallas_call | solution.py:488
  39.6 2.0 %shard_map.47 = f32[2,16,16,16,128]{4,3,2,1,0:T(8,128)} custom-call(f32[2,16,16,16,128]{4,3,2,1,0:T(8,128)S(1)} %shard_map.46.window), custom_call_target="tpu_custom_call" | custom-call | tf_op jit(solution)/shard_map/pallas_call | solution.py:536

commit v5 on v4

--- a/solution.py
+++ b/solution.py
@@ -16,7 +16,7 @@
 INNER = (2, BS - 2)
 INNER_CUTS = (0, 1, 4, 8, 12)
 INNER_CHUNKS = len(INNER_CUTS) - 1
-CHUNKS = INNER_CHUNKS + 3
+CHUNKS = INNER_CHUNKS + 4
 Z0 = 8
 Z1 = Z0 + BS
 MESH = pl.DeviceIdType.MESH
@@ -27,7 +27,7 @@
     fields, weights, levels, nbrs, out,
     raw, wraw, lraw, nraw,
     cp, mp, ep, sf, ftz, turned_own, slab, slab2, ints, kap, wown, wnear, st0, st1, st2,
-    spk, rpk, spk_in, rpk_in, spk_mid, rpk_mid, spk_out, rpk_out,
+    spk, rpk, spk_in, rpk_in, spk_rim, rpk_rim, spk_mid, rpk_mid, spk_out, rpk_out,
     in_sem, face_send, face_recv, move_send, move_recv, sum_send, sum_recv, w_send, w_recv,
 ):
     me = lax.axis_index("curve")
@@ -130,10 +130,13 @@
         sems = move_send.at[d, chunk], move_recv.at[slot, chunk]
         if chunk < INNER_CHUNKS:
             planes = pl.ds(INNER_CUTS[chunk], INNER_CUTS[chunk + 1] - INNER_CUTS[chunk])
-            return spk_in.at[d, planes], rpk_in.at[slot, planes], *sems
+            cut = planes, slice(None), slice(None), pl.ds(2, 12)
+            return spk_in.at[d, *cut], rpk_in.at[slot, *cut], *sems
         if chunk == INNER_CHUNKS:
+            return spk_rim.at[d], rpk_rim.at[slot], *sems
+        if chunk == INNER_CHUNKS + 1:
             return spk_mid.at[d], rpk_mid.at[slot], *sems
-        planes = pl.ds(2 * (chunk - INNER_CHUNKS - 1), 2)
+        planes = pl.ds(2 * (chunk - INNER_CHUNKS - 2), 2)
         return spk_out.at[d, planes], rpk_out.at[slot, planes], *sems
 
     kinds = [("face", step, pair) for step in range(2) for pair in range(3)]
@@ -329,9 +332,10 @@
     take_faces(0, 0)
     take_faces(0, 1)
 
-    @pl.loop(*INNER)
-    def _(x):
-        renew(x, RIM)
+    @pl.loop(1, BS // 2 - 1)
+    def _(k):
+        renew(2 * k, RIM)
+        renew(2 * k + 1, RIM)
 
     for x in RIM:
         renew(x, range(BS))
@@ -340,17 +344,13 @@
     pack_pair(1, 2)
     send_faces(1)
     potentials()
-    before, whole = take_sums(0, sums0)
-    st1[0:1] = whole
-    sums1 = send_sums(1)
-    take_faces(1, 2)
 
     turns = (0, 64, 32, 96)
 
     def quad(yy):
         return RIM if yy == 3 else tuple(2 + yy + 3 * j for j in range(4))
 
-    def evolve(x, groups, packed, plane):
+    def evolve(x, groups, packed, plane, ends=False):
         for comp, update in ((0, next_c), (1, next_s)):
             for some in (groups[:2], groups[2:]):
                 quads = [[update(x, y) for y in quad(yy)] for yy in some]
@@ -359,8 +359,14 @@
                 for i, yy in enumerate(some):
                     u0, u1, u2, u3 = turned[i]
                     row = groups.index(yy)
-                    packed[0, plane, comp, row] = jnp.where(slot32 == 0, u0, jnp.where(slot32 == 2, u1, jnp.where(slot32 == 1, u2, u3)))
-                    packed[1, plane, comp, row] = jnp.where(slot32 == 1, u0, jnp.where(slot32 == 3, u1, jnp.where(slot32 == 2, u2, u3)))
+                    to_left = jnp.where(slot32 == 0, u0, jnp.where(slot32 == 2, u1, jnp.where(slot32 == 1, u2, u3)))
+                    to_right = jnp.where(slot32 == 1, u0, jnp.where(slot32 == 3, u1, jnp.where(slot32 == 2, u2, u3)))
+                    for d, rows in ((0, to_left), (1, to_right)):
+                        if ends:
+                            packed[d, plane, row, 4 * comp : 4 * comp + 2] = rows[0:2]
+                            packed[d, plane, row, 4 * comp + 2 : 4 * comp + 4] = rows[BS - 2 : BS]
+                        else:
+                            packed[d, plane, comp, row] = rows
                     for j, y in enumerate(quad(yy)):
                         out[comp, x, y] = shown[i][j]
 
@@ -372,6 +378,16 @@
 
         send_sides(("move", chunk))
 
+    before, whole = take_sums(0, sums0)
+    st1[0:1] = whole
+    sums1 = send_sums(1)
+    take_faces(1, 2)
+
+    @pl.loop(0, 12)
+    def _(plane):
+        evolve(plane + 2, (0, 1, 2), spk_rim, plane, ends=True)
+
+    send_sides(("move", INNER_CHUNKS))
     before1, whole = take_sums(1, sums1)
     st2[0:1] = whole
     sums2 = send_sums(2)
@@ -379,15 +395,16 @@
     take_faces(1, 0)
     take_faces(1, 1)
 
-    @pl.loop(0, 12)
-    def _(plane):
-        evolve(plane + 2, (3,), spk_mid, plane)
-
-    send_sides(("move", INNER_CHUNKS))
+    @pl.loop(0, 6)
+    def _(k):
+        evolve(2 * k + 2, (3,), spk_mid, 2 * k)
+        evolve(2 * k + 3, (3,), spk_mid, 2 * k + 1)
+
+    send_sides(("move", INNER_CHUNKS + 1))
     for part in range(2):
         for k in (2 * part, 2 * part + 1):
             evolve(RIM[k], (0, 1, 2, 3), spk_out, k)
-        send_sides(("move", INNER_CHUNKS + 1 + part))
+        send_sides(("move", INNER_CHUNKS + 2 + part))
 
     before2, total = take_sums(2, sums2)
     before = before + before2
@@ -436,21 +453,27 @@
             for y, value in merged:
                 out[comp, x, y] = value
 
-    for chunk in range(INNER_CHUNKS):
+    for chunk in range(INNER_CHUNKS + 1):
         take_sides(("move", chunk))
-
-        @pl.loop(INNER_CUTS[chunk], INNER_CUTS[chunk + 1])
-        def _(plane):
-            settle(plane + 2, (0, 1, 2), rpk_in, plane)
-
-    take_sides(("move", INNER_CHUNKS))
 
     @pl.loop(0, 12)
     def _(plane):
-        settle(plane + 2, (3,), rpk_mid, plane)
+        for slot in range(2):
+            for comp in range(2):
+                for row in range(3):
+                    rpk_in[slot, plane, comp, row, 0:2] = rpk_rim[slot, plane, row, 4 * comp : 4 * comp + 2]
+                    rpk_in[slot, plane, comp, row, BS - 2 : BS] = rpk_rim[slot, plane, row, 4 * comp + 2 : 4 * comp + 4]
+        settle(plane + 2, (0, 1, 2), rpk_in, plane)
+
+    take_sides(("move", INNER_CHUNKS + 1))
+
+    @pl.loop(0, 6)
+    def _(k):
+        settle(2 * k + 2, (3,), rpk_mid, 2 * k)
+        settle(2 * k + 3, (3,), rpk_mid, 2 * k + 1)
 
     for part in range(2):
-        take_sides(("move", INNER_CHUNKS + 1 + part))
+        take_sides(("move", INNER_CHUNKS + 2 + part))
         for k in (2 * part, 2 * part + 1):
             settle(RIM[k], (0, 1, 2, 3), rpk_out, k)
 
@@ -514,6 +537,8 @@
             v((2, 3, 6, 3, 2, BS, 128), F32),
             v((2, 12, 2, 3, BS, 128), F32),
             v((3, 12, 2, 3, BS, 128), F32),
+            v((2, 12, 3, 8, 128), F32),
+            v((3, 12, 3, 8, 128), F32),
             v((2, 12, 2, 1, BS, 128), F32),
             v((3, 12, 2, 1, BS, 128), F32),
             v((2, 4, 2, 4, BS, 128), F32),

time: 41.7 us -> 39 us (0.935)
  Pallas kernels: 41.6 us -> 38.9 us
    pallas_call x1, Pallas kernels: 39.6 us -> 36.8 us  [body(): pl.pallas_call(kernel, out_shape=pltpu.VMEM((2, BS, BS, BS, 2 * PER), F32...]
where the time goes in v5:
time: 39 us; the launch traced here: 38.9 us
  Pallas kernels  38.9 us (100%)
    pallas_call x1, Pallas kernels, body(): pl.pallas_call(kernel, out_shape=pltpu.VMEM((2, BS, BS, BS, 2 * PER), F32...  36.8 us
    pallas_call x1, Pallas kernels, body(): pl.pallas_call(store_kernel, out_shape=jax.ShapeDtypeStruct((2, BS, BS, B...  2.04 us

profile of v5, /device:TPU:6, one launch (start us, length us, event | category | flops | bytes accessed | tf_op | source)
XLA Modules:
  0.0 38.9 jit_solution(13714281968749741427)
XLA Ops:
  0.0 36.8 %shard_map.46.window = f32[2,16,16,16,128]{4,3,2,1,0:T(8,128)S(1)} custom-call(f32[2,16,16,16,64]{4,3,2,1,0:T(8,128)} %fields.1, s32[1,64]{1,0:T(1,128)} %bitcast.2, s32[1,64]{1,0:T(1,128)} %bitcast.3, s32[6,64]{1,0:T(8,128)} %nbrs.1), custom_call_target="tpu_custom_call" | custom-call | flops 40000000 | bytes 8388608 | tf_op jit(solution)/shard_map/pallas_call | solution.py:511
  36.8 2.0 %shard_map.47 = f32[2,16,16,16,128]{4,3,2,1,0:T(8,128)} custom-call(f32[2,16,16,16,128]{4,3,2,1,0:T(8,128)S(1)} %shard_map.46.window), custom_call_target="tpu_custom_call" | custom-call | tf_op jit(solution)/shard_map/pallas_call | solution.py:561

commit v6 on v5

--- a/solution.py
+++ b/solution.py
@@ -291,12 +291,6 @@
     def next_s(x, y):
         return sf[x, y] + s_rate * (around_of(ep, x, y) - 6.0 * ep[x + 1, y + 1, Z0:Z1])
 
-    def send_faces(step):
-        send_sides(("face", step, 2))
-        for pair in (0, 1):
-            pack_pair(step, pair)
-            send_sides(("face", step, pair))
-
     def take_faces(step, pair):
         take_sides(("face", step, pair))
         ghost_face(step, 2 * pair)
@@ -310,7 +304,10 @@
     draw_z()
     pack_pair(0, 2)
     pl.semaphore_wait(barrier, PARTNERS + 2 + spare.astype(jnp.int32) - (first | last).astype(jnp.int32))
-    send_faces(0)
+    send_sides(("face", 0, 2))
+    for pair in (0, 1):
+        pack_pair(0, pair)
+        send_sides(("face", 0, pair))
     send_sides(("weights",))
     potentials()
     sums0 = send_sums(0)
@@ -332,17 +329,22 @@
     take_faces(0, 0)
     take_faces(0, 1)
 
+    for x in RIM:
+        renew(x, range(BS))
+
+    pack_pair(1, 0)
+    send_sides(("face", 1, 0))
+
     @pl.loop(1, BS // 2 - 1)
     def _(k):
         renew(2 * k, RIM)
         renew(2 * k + 1, RIM)
 
-    for x in RIM:
-        renew(x, range(BS))
-
     draw_z()
-    pack_pair(1, 2)
-    send_faces(1)
+    for pair in (2, 1):
+        pack_pair(1, pair)
+        send_sides(("face", 1, pair))
+
     potentials()
 
     turns = (0, 64, 32, 96)
@@ -381,6 +383,7 @@
     before, whole = take_sums(0, sums0)
     st1[0:1] = whole
     sums1 = send_sums(1)
+    take_faces(1, 0)
     take_faces(1, 2)
 
     @pl.loop(0, 12)
@@ -388,19 +391,18 @@
         evolve(plane + 2, (0, 1, 2), spk_rim, plane, ends=True)
 
     send_sides(("move", INNER_CHUNKS))
+    take_faces(1, 1)
+
+    @pl.loop(0, 6)
+    def _(k):
+        evolve(2 * k + 2, (3,), spk_mid, 2 * k)
+        evolve(2 * k + 3, (3,), spk_mid, 2 * k + 1)
+
+    send_sides(("move", INNER_CHUNKS + 1))
     before1, whole = take_sums(1, sums1)
     st2[0:1] = whole
     sums2 = send_sums(2)
     before = before + before1
-    take_faces(1, 0)
-    take_faces(1, 1)
-
-    @pl.loop(0, 6)
-    def _(k):
-        evolve(2 * k + 2, (3,), spk_mid, 2 * k)
-        evolve(2 * k + 3, (3,), spk_mid, 2 * k + 1)
-
-    send_sides(("move", INNER_CHUNKS + 1))
     for part in range(2):
         for k in (2 * part, 2 * part + 1):
             evolve(RIM[k], (0, 1, 2, 3), spk_out, k)

time: 39 us -> 38.9 us (level)
  no operation moved by 1% of the time
where the time goes in v6:
time: 38.9 us; the launch traced here: 38.8 us
  Pallas kernels  38.8 us (100%)
    pallas_call x1, Pallas kernels, body(): pl.pallas_call(kernel, out_shape=pltpu.VMEM((2, BS, BS, BS, 2 * PER), F32...  36.8 us
    pallas_call x1, Pallas kernels, body(): pl.pallas_call(store_kernel, out_shape=jax.ShapeDtypeStruct((2, BS, BS, B...  2.04 us

profile of v6, /device:TPU:6, one launch (start us, length us, event | category | flops | bytes accessed | tf_op | source)
XLA Modules:
  0.0 38.8 jit_solution(10314194052544171146)
XLA Ops:
  0.0 36.8 %shard_map.46.window = f32[2,16,16,16,128]{4,3,2,1,0:T(8,128)S(1)} custom-call(f32[2,16,16,16,64]{4,3,2,1,0:T(8,128)} %fields.1, s32[1,64]{1,0:T(1,128)} %bitcast.2, s32[1,64]{1,0:T(1,128)} %bitcast.3, s32[6,64]{1,0:T(8,128)} %nbrs.1), custom_call_target="tpu_custom_call" | custom-call | flops 40000000 | bytes 8388608 | tf_op jit(solution)/shard_map/pallas_call | solution.py:513
  36.8 2.0 %shard_map.47 = f32[2,16,16,16,128]{4,3,2,1,0:T(8,128)} custom-call(f32[2,16,16,16,128]{4,3,2,1,0:T(8,128)S(1)} %shard_map.46.window), custom_call_target="tpu_custom_call" | custom-call | tf_op jit(solution)/shard_map/pallas_call | solution.py:563
